TPU v7x, 32 devices: a whole 2x2x4 slice. The times are simulated.
32 devices in a mesh: dp: 8 (over y, x, core), fsdp: 4 (over z).
Axes of the slice: x: 2, y: 2, z: 4, core: 2. Of those that a mesh axis runs over, the one named last changes fastest.
Arguments:
- tokens: bfloat16 [32768, 384], P(('dp', 'fsdp')), may hold values from -6 to 6
- cotangent: bfloat16 [32768, 384], P(('dp', 'fsdp')), may hold values from -6 to 6
- prefix_len: int32 [32], P(('dp', 'fsdp')), may hold values from 64 to 256, as said below
- valid_len: int32 [32], P(('dp', 'fsdp')), may hold values from 512 to 1024, as said below
- qkv_weight: float32 [2, 384, 1152], P(None, 'fsdp'), may hold values from -0.3125 to 0.3125
- qkv_first: float32 [2, 384, 1152], P(None, 'fsdp'), may hold values from -256 to 256
- qkv_second: float32 [2, 384, 1152], P(None, 'fsdp'), may hold values from 655.36 to 5242.88
- proj_weight: float32 [2, 384, 384], P(None, 'fsdp'), may hold values from -6 to 6
- proj_first: float32 [2, 384, 384], P(None, 'fsdp'), may hold values from -6 to 6
- proj_second: float32 [2, 384, 384], P(None, 'fsdp'), may hold values from 0.64 to 5.12
- up_weight: float32 [2, 384, 1536], P(None, 'fsdp'), may hold values from -0.3125 to 0.3125
- up_first: float32 [2, 384, 1536], P(None, 'fsdp'), may hold values from -32 to 32
- up_second: float32 [2, 384, 1536], P(None, 'fsdp'), may hold values from 9.8304 to 81.92
- down_weight: float32 [2, 1536, 384], P(None, 'fsdp'), may hold values from -0.15625 to 0.15625
- down_first: float32 [2, 1536, 384], P(None, 'fsdp'), may hold values from -64 to 64
- down_second: float32 [2, 1536, 384], P(None, 'fsdp'), may hold values from 40.96 to 327.68
- norm_gains: float32 [2, 2, 384], P(None, None, 'fsdp'), may hold values from 0.5 to 1.5
- gains_first: float32 [2, 2, 384], P(None, None, 'fsdp'), may hold values from -256 to 256
- gains_second: float32 [2, 2, 384], P(None, None, 'fsdp'), may hold values from 655.36 to 5242.88
Outputs:
- block_out: bfloat16 [32768, 384], P(('dp', 'fsdp'))
- tokens_grad: bfloat16 [32768, 384], P(('dp', 'fsdp'))
- qkv_first_new: float32 [2, 384, 1152], P(None, 'fsdp')
- qkv_second_new: float32 [2, 384, 1152], P(None, 'fsdp')
- qkv_new: float32 [2, 384, 1152], P(None, 'fsdp')
- proj_first_new: float32 [2, 384, 384], P(None, 'fsdp')
- proj_second_new: float32 [2, 384, 384], P(None, 'fsdp')
- proj_new: float32 [2, 384, 384], P(None, 'fsdp')
- up_first_new: float32 [2, 384, 1536], P(None, 'fsdp')
- up_second_new: float32 [2, 384, 1536], P(None, 'fsdp')
- up_new: float32 [2, 384, 1536], P(None, 'fsdp')
- down_first_new: float32 [2, 1536, 384], P(None, 'fsdp')
- down_second_new: float32 [2, 1536, 384], P(None, 'fsdp')
- down_new: float32 [2, 1536, 384], P(None, 'fsdp')
- gains_first_new: float32 [2, 2, 384], P(None, None, 'fsdp')
- gains_second_new: float32 [2, 2, 384], P(None, None, 'fsdp')
- gains_new: float32 [2, 2, 384], P(None, None, 'fsdp')
Inputs may be any that keep to these rules, and one draw needn't show every extreme that they name: `prefix_len`: every sequence has a prefix shorter than its valid length; some sequence has a prefix of 256 tokens. `valid_len`: some sequence has no padding.
All inputs are finite; a program needn't handle non-finite values.
Results may differ from a plain program's by a relative error of at most 0.025.
The roundings to bfloat16 on the way count: a program that leaves them out, or rounds other values in their place, can miss the bound.
Values may be sent and summed in bfloat16 or wider, within the bound.
A program may use at most 192 MiB of HBM per device.

v0:
```python
import math

import jax
import jax.numpy as jnp
from jax import lax
from jax.sharding import PartitionSpec as P

D = 384
HEADS = 6
HEAD_DIM = 64
FF = 1536
SEQ = 1024
STEP_COUNT = 7


NEG_FILL = -1e30
EPS_NORM = 1e-05
EPS_ADAM = 1e-08
BETA_ONE = 0.9
BETA_TWO = 0.99


def layer_norm(values):
    average = jnp.mean(values, axis=-1, keepdims=True)
    centered = values - average
    inverse = lax.rsqrt(jnp.mean(centered * centered, axis=-1, keepdims=True) + EPS_NORM)
    return (centered * inverse, inverse)


def norm_backward(grad_out, normed, inverse, gain):
    scaled = grad_out * gain
    gain_grad = jnp.sum(grad_out * normed, axis=0)
    grad_in = inverse * (
        scaled
        - jnp.mean(scaled, axis=-1, keepdims=True)
        - normed * jnp.mean(scaled * normed, axis=-1, keepdims=True)
    )
    return (grad_in, gain_grad)


def gelu_exact(values):
    return jax.nn.gelu(values, approximate=False)


def block_allowed(block_start, row_count, length, prefix, valid):
    rows_at = block_start + jnp.arange(row_count, dtype=jnp.int32)
    cols_at = jnp.arange(length, dtype=jnp.int32)
    return (cols_at[None, :] < valid) & (
        (cols_at[None, :] <= rows_at[:, None]) | (cols_at[None, :] < prefix)
    )


def block_scores(query_rows, key_rows, allowed, score_scale):
    scores = (
        jnp.einsum("qhd,khd->hqk", query_rows, key_rows, preferred_element_type=jnp.float32)
        * score_scale
    )
    return jnp.where(allowed[None], scores, NEG_FILL)


def attend_forward(queries, keys, values, prefix_len, valid_len):
    seq_count, length, head_count, head_width = queries.shape
    row_count = min(512, length)
    score_scale = head_width ** (-0.5)

    def per_sequence(query_rows, key_rows, value_rows, prefix, valid, block_start):
        allowed = block_allowed(block_start, row_count, length, prefix, valid)
        scores = block_scores(query_rows, key_rows, allowed, score_scale)
        largest = jnp.max(scores, axis=-1, keepdims=True)
        exponent = jnp.exp(scores - largest)
        denominator = jnp.sum(exponent, axis=-1, keepdims=True)
        soft_probs = (exponent / denominator).astype(jnp.bfloat16)
        mixed = jnp.einsum(
            "hqk,khd->qhd", soft_probs, value_rows, preferred_element_type=jnp.float32
        )
        return (mixed.astype(jnp.bfloat16), (largest + jnp.log(denominator))[..., 0])

    def step_block(block_index, carry):
        mixed_all, total_all = carry
        block_start = block_index * row_count
        query_rows = lax.dynamic_slice_in_dim(queries, block_start, row_count, 1)
        mixed, log_total = jax.vmap(per_sequence, in_axes=(0, 0, 0, 0, 0, None))(
            query_rows, keys, values, prefix_len, valid_len, block_start
        )
        mixed_all = lax.dynamic_update_slice_in_dim(mixed_all, mixed, block_start, 1)
        total_all = lax.dynamic_update_slice_in_dim(total_all, log_total, block_start, 2)
        return (mixed_all, total_all)

    start_state = (
        jnp.zeros(queries.shape, jnp.bfloat16),
        jnp.zeros((seq_count, head_count, length), jnp.float32),
    )
    return lax.fori_loop(0, length // row_count, step_block, start_state)


def attend_backward(queries, keys, values, grad_mixed, log_total, prefix_len, valid_len):
    seq_count, length, head_count, head_width = queries.shape
    row_count = min(512, length)
    score_scale = head_width ** (-0.5)

    def per_sequence(
        query_rows, grad_rows, total_rows, key_rows, value_rows, prefix, valid, block_start
    ):
        allowed = block_allowed(block_start, row_count, length, prefix, valid)
        scores = block_scores(query_rows, key_rows, allowed, score_scale)
        soft_probs = jnp.exp(scores - total_rows[..., None])
        grad_probs = jnp.einsum(
            "qhd,khd->hqk", grad_rows, value_rows, preferred_element_type=jnp.float32
        )
        grad_scores = (
            soft_probs * (grad_probs - jnp.sum(grad_probs * soft_probs, axis=-1, keepdims=True))
        ).astype(jnp.bfloat16)
        query_part = (
            jnp.einsum("hqk,khd->qhd", grad_scores, key_rows, preferred_element_type=jnp.float32)
            * score_scale
        )
        key_part = (
            jnp.einsum("hqk,qhd->khd", grad_scores, query_rows, preferred_element_type=jnp.float32)
            * score_scale
        )
        value_part = jnp.einsum(
            "hqk,qhd->khd",
            soft_probs.astype(jnp.bfloat16),
            grad_rows,
            preferred_element_type=jnp.float32,
        )
        return (query_part, key_part, value_part)

    def step_block(block_index, carry):
        query_grads, key_grads, value_grads = carry
        block_start = block_index * row_count
        query_rows = lax.dynamic_slice_in_dim(queries, block_start, row_count, 1)
        grad_rows = lax.dynamic_slice_in_dim(grad_mixed, block_start, row_count, 1)
        total_rows = lax.dynamic_slice_in_dim(log_total, block_start, row_count, 2)
        query_part, key_part, value_part = jax.vmap(
            per_sequence, in_axes=(0, 0, 0, 0, 0, 0, 0, None)
        )(query_rows, grad_rows, total_rows, keys, values, prefix_len, valid_len, block_start)
        query_grads = lax.dynamic_update_slice_in_dim(query_grads, query_part, block_start, 1)
        return (query_grads, key_grads + key_part, value_grads + value_part)

    zero_grads = jnp.zeros(queries.shape, jnp.float32)
    return lax.fori_loop(0, length // row_count, step_block, (zero_grads, zero_grads, zero_grads))


def adam_step(weight, first_moment, second, gradient, step_rate, weight_decay):
    first_new = BETA_ONE * first_moment + (1.0 - BETA_ONE) * gradient
    second_new = BETA_TWO * second + (1.0 - BETA_TWO) * gradient * gradient
    first_fix = 1.0 - BETA_ONE**STEP_COUNT
    second_fix = 1.0 - BETA_TWO**STEP_COUNT
    update = first_new / first_fix / (jnp.sqrt(second_new / second_fix) + EPS_ADAM)
    return (first_new, second_new, weight - step_rate * (update + weight_decay * weight))


def per_device(
    tokens,
    cotangent,
    prefix_len,
    valid_len,
    qkv_weight,
    qkv_first,
    qkv_second,
    proj_weight,
    proj_first,
    proj_second,
    up_weight,
    up_first,
    up_second,
    down_weight,
    down_first,
    down_second,
    norm_gains,
    gains_first,
    gains_second,
):
    tok_rows, model_width = tokens.shape
    seq_count = prefix_len.shape[0]
    length = tok_rows // seq_count
    layers = qkv_weight.shape[0]
    stream = tokens.astype(jnp.float32)
    kept_weights = []
    kept_saved = []
    for layer_index in range(layers):
        fetched = (
            lax.all_gather(
                qkv_weight[layer_index].astype(jnp.bfloat16), "fsdp", axis=0, tiled=True
            ),
            lax.all_gather(
                proj_weight[layer_index].astype(jnp.bfloat16), "fsdp", axis=0, tiled=True
            ),
            lax.all_gather(up_weight[layer_index].astype(jnp.bfloat16), "fsdp", axis=0, tiled=True),
            lax.all_gather(
                down_weight[layer_index].astype(jnp.bfloat16), "fsdp", axis=0, tiled=True
            ),
            lax.all_gather(
                norm_gains[layer_index].astype(jnp.bfloat16), "fsdp", axis=1, tiled=True
            ),
        )
        forward_w_qkv, forward_w_proj, forward_w_up, forward_w_down, forward_gain_pair = fetched
        forward_gain_one = forward_gain_pair[0].astype(jnp.float32)
        forward_gain_two = forward_gain_pair[1].astype(jnp.float32)
        forward_normed_one, forward_inverse_one = layer_norm(stream)
        forward_attn_in = (forward_normed_one * forward_gain_one).astype(jnp.bfloat16)
        qkv_rows = jnp.dot(
            forward_attn_in, forward_w_qkv, preferred_element_type=jnp.float32
        ).astype(jnp.bfloat16)
        split = qkv_rows.reshape(seq_count, length, 3, HEADS, HEAD_DIM)
        forward_queries = split[:, :, 0]
        forward_keys = split[:, :, 1]
        forward_values = split[:, :, 2]
        mixed, forward_log_total = attend_forward(
            forward_queries, forward_keys, forward_values, prefix_len, valid_len
        )
        forward_mixed_rows = mixed.reshape(tok_rows, model_width)
        middle = stream + jnp.dot(
            forward_mixed_rows, forward_w_proj, preferred_element_type=jnp.float32
        )
        forward_normed_two, forward_inverse_two = layer_norm(middle)
        forward_ffn_in = (forward_normed_two * forward_gain_two).astype(jnp.bfloat16)
        forward_hidden_pre = jnp.dot(
            forward_ffn_in, forward_w_up, preferred_element_type=jnp.float32
        )
        forward_hidden = gelu_exact(forward_hidden_pre).astype(jnp.bfloat16)
        result = middle + jnp.dot(
            forward_hidden, forward_w_down, preferred_element_type=jnp.float32
        )
        forward_saved = (
            forward_normed_one,
            forward_inverse_one,
            forward_attn_in,
            forward_queries,
            forward_keys,
            forward_values,
            forward_log_total,
            forward_mixed_rows,
            forward_normed_two,
            forward_inverse_two,
            forward_ffn_in,
            forward_hidden_pre,
            forward_hidden,
        )
        stream = result
        kept_weights.append(fetched)
        kept_saved.append(forward_saved)
    block_out = stream.astype(jnp.bfloat16)
    positions = jnp.arange(length, dtype=jnp.int32)
    live = (positions[None, :] < valid_len[:, None]).reshape(tok_rows, 1)
    grad_stream = jnp.where(live, cotangent.astype(jnp.float32), jnp.float32(0.0))
    layer_shards = [None] * layers
    for layer_index in reversed(range(layers)):
        fetched = (
            lax.all_gather(
                qkv_weight[layer_index].astype(jnp.bfloat16), "fsdp", axis=0, tiled=True
            ),
            lax.all_gather(
                proj_weight[layer_index].astype(jnp.bfloat16), "fsdp", axis=0, tiled=True
            ),
            lax.all_gather(up_weight[layer_index].astype(jnp.bfloat16), "fsdp", axis=0, tiled=True),
            lax.all_gather(
                down_weight[layer_index].astype(jnp.bfloat16), "fsdp", axis=0, tiled=True
            ),
            lax.all_gather(
                norm_gains[layer_index].astype(jnp.bfloat16), "fsdp", axis=1, tiled=True
            ),
        )
        w_qkv, w_proj, w_up, w_down, gain_pair = fetched
        gain_one = gain_pair[0].astype(jnp.float32)
        gain_two = gain_pair[1].astype(jnp.float32)
        (
            normed_one,
            inverse_one,
            attn_in,
            queries,
            keys,
            values,
            log_total,
            mixed_rows,
            normed_two,
            inverse_two,
            ffn_in,
            hidden_pre,
            hidden,
        ) = kept_saved[layer_index]
        grad_ffn = grad_stream.astype(jnp.bfloat16)
        down_grad = jnp.einsum("tf,td->fd", hidden, grad_ffn, preferred_element_type=jnp.float32)
        grad_hidden = jnp.einsum("td,fd->tf", grad_ffn, w_down, preferred_element_type=jnp.float32)
        slope_back = jax.vjp(gelu_exact, hidden_pre)[1]
        grad_pre = slope_back(grad_hidden)[0].astype(jnp.bfloat16)
        up_grad = jnp.einsum("td,tf->df", ffn_in, grad_pre, preferred_element_type=jnp.float32)
        grad_ffn_in = jnp.einsum("tf,df->td", grad_pre, w_up, preferred_element_type=jnp.float32)
        grad_middle_norm, gain_two_grad = norm_backward(
            grad_ffn_in, normed_two, inverse_two, gain_two
        )
        grad_middle = grad_stream + grad_middle_norm
        grad_attn = grad_middle.astype(jnp.bfloat16)
        proj_grad = jnp.einsum(
            "td,te->de", mixed_rows, grad_attn, preferred_element_type=jnp.float32
        )
        grad_mixed = jnp.einsum(
            "te,de->td", grad_attn, w_proj, preferred_element_type=jnp.float32
        ).astype(jnp.bfloat16)
        grad_mixed = grad_mixed.reshape(seq_count, length, HEADS, HEAD_DIM)
        query_grads, key_grads, value_grads = attend_backward(
            queries, keys, values, grad_mixed, log_total, prefix_len, valid_len
        )
        grad_qkv = (
            jnp.stack((query_grads, key_grads, value_grads), axis=2)
            .reshape(tok_rows, 3 * model_width)
            .astype(jnp.bfloat16)
        )
        qkv_grad = jnp.einsum("td,te->de", attn_in, grad_qkv, preferred_element_type=jnp.float32)
        grad_attn_in = jnp.einsum("te,de->td", grad_qkv, w_qkv, preferred_element_type=jnp.float32)
        grad_stream_norm, gain_one_grad = norm_backward(
            grad_attn_in, normed_one, inverse_one, gain_one
        )
        gains_grad = jnp.stack((gain_one_grad, gain_two_grad))
        grad_stream = grad_middle + grad_stream_norm
        grads = (qkv_grad, proj_grad, up_grad, down_grad, gains_grad)
        shards = (
            lax.psum_scatter(
                grads[0].astype(jnp.bfloat16), "fsdp", scatter_dimension=0, tiled=True
            ).astype(jnp.float32),
            lax.psum_scatter(
                grads[1].astype(jnp.bfloat16), "fsdp", scatter_dimension=0, tiled=True
            ).astype(jnp.float32),
            lax.psum_scatter(
                grads[2].astype(jnp.bfloat16), "fsdp", scatter_dimension=0, tiled=True
            ).astype(jnp.float32),
            lax.psum_scatter(
                grads[3].astype(jnp.bfloat16), "fsdp", scatter_dimension=0, tiled=True
            ).astype(jnp.float32),
            lax.psum_scatter(
                grads[4].astype(jnp.bfloat16), "fsdp", scatter_dimension=1, tiled=True
            ).astype(jnp.float32),
        )
        shards = lax.psum((shards[0], shards[1], shards[2], shards[3], shards[4]), "dp")
        layer_shards[layer_index] = shards
    tokens_grad = grad_stream.astype(jnp.bfloat16)
    stacked = tuple(
        (
            jnp.stack([layer_shards[layer_index][member] for layer_index in range(layers)])
            for member in range(5)
        )
    )
    masters = (qkv_weight, proj_weight, up_weight, down_weight, norm_gains)
    firsts = (qkv_first, proj_first, up_first, down_first, gains_first)
    seconds = (qkv_second, proj_second, up_second, down_second, gains_second)
    rates = (
        2.5 / math.sqrt(D),
        2.5 / math.sqrt(max(4 * D // SEQ, 1)),
        2.5 / math.sqrt(D),
        2.5 / math.sqrt(FF),
        0.5,
    )
    decays = (0.1, 0.1, 0.1, 0.1, 0.0)
    results = []
    for kind in range(5):
        results.extend(
            adam_step(
                masters[kind], firsts[kind], seconds[kind], stacked[kind], rates[kind], decays[kind]
            )
        )
    return (
        block_out,
        tokens_grad,
        results[0],
        results[1],
        results[2],
        results[3],
        results[4],
        results[5],
        results[6],
        results[7],
        results[8],
        results[9],
        results[10],
        results[11],
        results[12],
        results[13],
        results[14],
    )


def solution(mesh):
    return jax.shard_map(
        per_device,
        mesh=mesh,
        in_specs=(
            P(("dp", "fsdp"), None),
            P(("dp", "fsdp"), None),
            P(("dp", "fsdp")),
            P(("dp", "fsdp")),
            P(None, "fsdp", None),
            P(None, "fsdp", None),
            P(None, "fsdp", None),
            P(None, "fsdp", None),
            P(None, "fsdp", None),
            P(None, "fsdp", None),
            P(None, "fsdp", None),
            P(None, "fsdp", None),
            P(None, "fsdp", None),
            P(None, "fsdp", None),
            P(None, "fsdp", None),
            P(None, "fsdp", None),
            P(None, None, "fsdp"),
            P(None, None, "fsdp"),
            P(None, None, "fsdp"),
        ),
        out_specs=(
            P(("dp", "fsdp"), None),
            P(("dp", "fsdp"), None),
            P(None, "fsdp", None),
            P(None, "fsdp", None),
            P(None, "fsdp", None),
            P(None, "fsdp", None),
            P(None, "fsdp", None),
            P(None, "fsdp", None),
            P(None, "fsdp", None),
            P(None, "fsdp", None),
            P(None, "fsdp", None),
            P(None, "fsdp", None),
            P(None, "fsdp", None),
            P(None, "fsdp", None),
            P(None, None, "fsdp"),
            P(None, None, "fsdp"),
            P(None, None, "fsdp"),
        ),
        check_vma=False,
    )
```

profile of v0, /device:TPU:0, one launch (start us, length us, event | category | flops | bytes accessed | tf_op | source)
XLA Modules:
  0.0 686.5 jit_solution(16584568221265803512)
XLA Ops:
  13.4 16.2 %all-gather.5 = bf16[1,2,384]{1,0,2:T(2,128)(2,1)S(1)} all-gather(bf16[1,2,96]{1,0,2:T(2,128)(2,1)S(1)} %get-tuple-element.970), channel_id=7, replica_groups=mesh['dp'=8,'fsdp'=4] {'fsdp'}, dimensions={2}, use_global_device_ids=true | all-gather | bytes 1920 | tf_op jit(solution)/shard_map/all_gather | solution.py:194
  32.0 15.4 %all-gather = bf16[1,2,384]{1,0,2:T(2,128)(2,1)S(1)} all-gather(bf16[1,2,96]{1,0,2:T(2,128)(2,1)S(1)} %get-tuple-element.971), channel_id=2, replica_groups=mesh['dp'=8,'fsdp'=4] {'fsdp'}, dimensions={2}, use_global_device_ids=true | all-gather | bytes 1920 | tf_op jit(solution)/shard_map/all_gather | solution.py:194
  49.1 16.3 %all-gather.7 = bf16[1,384,384]{2,1,0:T(8,128)(2,1)} all-gather(bf16[1,96,384]{2,1,0:T(8,128)(2,1)S(1)} %get-tuple-element.968), channel_id=9, replica_groups=mesh['dp'=8,'fsdp'=4] {'fsdp'}, dimensions={1}, use_global_device_ids=true | all-gather | bytes 368640 | tf_op jit(solution)/shard_map/all_gather | solution.py:187
  65.4 18.2 %all-gather.2 = bf16[1,384,384]{2,1,0:T(8,128)(2,1)S(1)} all-gather(bf16[1,96,384]{2,1,0:T(8,128)(2,1)S(1)} %get-tuple-element.969), channel_id=4, replica_groups=mesh['dp'=8,'fsdp'=4] {'fsdp'}, dimensions={1}, use_global_device_ids=true | all-gather | bytes 368640 | tf_op jit(solution)/shard_map/all_gather | solution.py:187
  83.8 19.2 %all-gather.6 = bf16[1,384,1152]{2,1,0:T(8,128)(2,1)} all-gather(bf16[1,96,1152]{2,1,0:T(8,128)(2,1)S(1)} %get-tuple-element.966), channel_id=8, replica_groups=mesh['dp'=8,'fsdp'=4] {'fsdp'}, dimensions={1}, use_global_device_ids=true | all-gather | bytes 1105920 | tf_op jit(solution)/shard_map/all_gather | solution.py:184
  104.9 30.9 %all-gather.1 = bf16[1,384,1152]{2,1,0:T(8,128)(2,1)S(1)} all-gather(bf16[1,96,1152]{2,1,0:T(8,128)(2,1)S(1)} %get-tuple-element.967), channel_id=3, replica_groups=mesh['dp'=8,'fsdp'=4] {'fsdp'}, dimensions={1}, use_global_device_ids=true | all-gather | bytes 1105920 | tf_op jit(solution)/shard_map/all_gather | solution.py:184
  143.8 26.4 %while.66 = (s32[]{:T(128)}, bf16[1,1024,6,64]{1,3,2,0:T(8,128)(2,1)}, f32[1,6,1024]{2,1,0:T(8,128)S(1)}, s32[1]{0:T(128)}, s32[1]{0:T(128)}, /*index=5*/bf16[1,...) while((s32[]{:T(128)}, ...), condition=%wide.region_5.6_spmd, body=%wide.region_2.5_spmd.sunk | while | flops 844824064 | bytes 48623856 | solution.py:93
  174.1 19.0 %multiply_convert_fusion.3 = (bf16[1024,1536]{1,0:T(8,128)(2,1)}, f32[1024,1536]{1,0:T(8,128)}, f32[1024,1536]{1,0:T(8,128)}) fusion(bf16[1,384,1536]{2,1,0:T(8,128)(2,1)} %all-gather.15.cloned.1.call-done, f32[1024,384]{0,1:T(8,128)} %copy-done.21, f32[384]{0:T(512)S(1)} %get-tuple-element.833, f32[1024]{0:T(1024)S(1)} %add_rsqrt_fusion.2, ...), kind=kOutput, calls=%fused_computation.141 | convolution fusion | flops 1311768576 | bytes 18490880 | tf_op jit(solution)/shard_map/dot_general | solution.py:219
  204.2 24.7 %while.67 = (s32[]{:T(128)}, bf16[1,1024,6,64]{1,3,2,0:T(8,128)(2,1)S(1)}, f32[1,6,1024]{2,1,0:T(8,128)S(1)}, s32[1]{0:T(128)}, s32[1]{0:T(128)}, /*index=5*/bf1...) while((s32[]{:T(128)}, ...), condition=%wide.region_13.14_spmd, body=%wide.region_10.13_spmd.sunk | while | flops 844824064 | bytes 42332348 | solution.py:93
  232.7 19.2 %multiply_convert_fusion.2 = (bf16[1024,1536]{1,0:T(8,128)(2,1)}, f32[1024,1536]{1,0:T(8,128)}, f32[1024,1536]{1,0:T(8,128)}) fusion(bf16[1,384,1536]{2,1,0:T(8,128)(2,1)} %all-gather.19.cloned.1.call-done, f32[1024,384]{0,1:T(8,128)} %copy-done.16, f32[384]{0:T(512)S(1)} %copy-done.99, f32[1024]{0:T(1024)S(1)} %add_rsqrt_fusion, ...), kind=kOutput, calls=%fused_computation.128 | convolution fusion | flops 1311768576 | bytes 18490880 | tf_op jit(solution)/shard_map/dot_general | solution.py:219
  268.3 49.9 %while.68 = (s32[]{:T(128)}, bf16[1,1024,6,64]{1,3,2,0:T(8,128)(2,1)}, f32[1,1024,6,64]{1,3,2,0:T(8,128)S(1)}, f32[1,1024,6,64]{1,3,2,0:T(8,128)}, s32[1]{0:T(12...) while((s32[]{:T(128)}, ...), condition=%wide.region_20.21_spmd.clone, body=%wide.region_18.20_spmd.clone.sunk | while | flops 2064186880 | bytes 132747672 | solution.py:142
  275.6 7.1 %multiply_reduce_fusion.17 = (f32[6,512]{1,0:T(8,128)S(1)}, f32[6,512,1024]{2,1,0:T(8,128)}) fusion(f32[6,512,1024]{2,1,0:T(8,128)S(1)} %fusion.245, f32[6,512]{1,0:T(8,128)S(1)} %dynamic-slice_bitcast_fusion.4, pred[512,1024]{1,0:T(8,128)(4,1)S(1)} %fusion.246, bf16[1,1024,6,64]{1,3,2,0:T(8,128)(2,1)S(1)} %copy-done.9, ...), kind=kOutput, calls=%fused_computation.49.clone.1 | convolution fusion | flops 418378752 | bytes 26898436 | tf_op jit(solution)/shard_map/while/body/eval_jaxpr/vmap(qhd,khd->hqk)/dot_general | solution.py:107
  300.4 7.1 %multiply_reduce_fusion.17 = (f32[6,512]{1,0:T(8,128)S(1)}, f32[6,512,1024]{2,1,0:T(8,128)}) fusion(f32[6,512,1024]{2,1,0:T(8,128)S(1)} %fusion.245, f32[6,512]{1,0:T(8,128)S(1)} %dynamic-slice_bitcast_fusion.4, pred[512,1024]{1,0:T(8,128)(4,1)S(1)} %fusion.246, bf16[1,1024,6,64]{1,3,2,0:T(8,128)(2,1)S(1)} %copy-done.9, ...), kind=kOutput, calls=%fused_computation.49.clone.1 | convolution fusion | flops 418378752 | bytes 26898436 | tf_op jit(solution)/shard_map/while/body/eval_jaxpr/vmap(qhd,khd->hqk)/dot_general | solution.py:107
  343.0 50.2 %while.69 = (s32[]{:T(128)}, bf16[1,1024,6,64]{1,3,2,0:T(8,128)(2,1)}, f32[1,1024,6,64]{1,3,2,0:T(8,128)S(1)}, f32[1,1024,6,64]{1,3,2,0:T(8,128)}, s32[1]{0:T(12...) while((s32[]{:T(128)}, ...), condition=%wide.region_27.28_spmd.clone, body=%wide.region_25.27_spmd.clone.sunk | while | flops 2064186880 | bytes 132747672 | solution.py:142
  350.6 7.1 %multiply_reduce_fusion.18 = (f32[6,512]{1,0:T(8,128)S(1)}, f32[6,512,1024]{2,1,0:T(8,128)}) fusion(f32[6,512,1024]{2,1,0:T(8,128)S(1)} %fusion.256, f32[6,512]{1,0:T(8,128)S(1)} %dynamic-slice_bitcast_fusion.5, pred[512,1024]{1,0:T(8,128)(4,1)S(1)} %fusion.257, bf16[1,1024,6,64]{1,3,2,0:T(8,128)(2,1)S(1)} %copy-done.7, ...), kind=kOutput, calls=%fused_computation.86.clone.1 | convolution fusion | flops 418378752 | bytes 26898436 | tf_op jit(solution)/shard_map/while/body/eval_jaxpr/vmap(qhd,khd->hqk)/dot_general | solution.py:107
  375.5 7.1 %multiply_reduce_fusion.18 = (f32[6,512]{1,0:T(8,128)S(1)}, f32[6,512,1024]{2,1,0:T(8,128)}) fusion(f32[6,512,1024]{2,1,0:T(8,128)S(1)} %fusion.256, f32[6,512]{1,0:T(8,128)S(1)} %dynamic-slice_bitcast_fusion.5, pred[512,1024]{1,0:T(8,128)(4,1)S(1)} %fusion.257, bf16[1,1024,6,64]{1,3,2,0:T(8,128)(2,1)S(1)} %copy-done.7, ...), kind=kOutput, calls=%fused_computation.86.clone.1 | convolution fusion | flops 418378752 | bytes 26898436 | tf_op jit(solution)/shard_map/while/body/eval_jaxpr/vmap(qhd,khd->hqk)/dot_general | solution.py:107
  431.7 22.9 %reduce-scatter.29.cloned.1.call-done = bf16[384,384]{1,0:T(8,128)(2,1)} async-done(((bf16[1536,384]{1,0:T(8,128)(2,1)}), bf16[384,384]{1,0:T(8,128)(2,1)}) %reduce-scatter.29.cloned.1.call-update) | async-done | bytes 294928 | tf_op jit(solution)/shard_map/reduce_scatter | solution.py:328
  456.5 28.8 %reduce-scatter.25.cloned.1.call-done = bf16[96,1536]{1,0:T(8,128)(2,1)} async-done(((bf16[384,1536]{1,0:T(8,128)(2,1)}), bf16[96,1536]{1,0:T(8,128)(2,1)}) %reduce-scatter.25.cloned.1.call-update) | async-done | bytes 294928 | tf_op jit(solution)/shard_map/reduce_scatter | solution.py:325
  487.1 29.0 %reduce-scatter.23.cloned.1.call-done = bf16[96,1536]{1,0:T(8,128)(2,1)} async-done(((bf16[384,1536]{1,0:T(8,128)(2,1)}), bf16[96,1536]{1,0:T(8,128)(2,1)}) %reduce-scatter.23.cloned.1.call-update) | async-done | bytes 294928 | tf_op jit(solution)/shard_map/reduce_scatter | solution.py:325
  517.9 28.8 %reduce-scatter.27.cloned.1.call-done = bf16[384,384]{1,0:T(8,128)(2,1)} async-done(((bf16[1536,384]{1,0:T(8,128)(2,1)}), bf16[384,384]{1,0:T(8,128)(2,1)}) %reduce-scatter.27.cloned.1.call-update) | async-done | bytes 294928 | tf_op jit(solution)/shard_map/reduce_scatter | solution.py:328
  557.1 9.8 %reduce-scatter.33.cloned.1.call-done = bf16[96,2]{1,0:T(8,128)(2,1)} async-done(((bf16[384,2]{1,0:T(8,128)(2,1)}), bf16[96,2]{1,0:T(8,128)(2,1)}) %reduce-scatter.33.cloned.1.call-update) | async-done | bytes 400
  567.7 19.3 %reduce-scatter.31.cloned.1.call-done = bf16[96,2]{1,0:T(8,128)(2,1)} async-done(((bf16[384,2]{1,0:T(8,128)(2,1)}), bf16[96,2]{1,0:T(8,128)(2,1)}) %reduce-scatter.31.cloned.1.call-update) | async-done | bytes 400
  587.8 12.2 %all-reduce = (f32[1,2,96]{2,1,0:T(2,128)S(1)}, f32[1,2,96]{2,1,0:T(2,128)S(1)}) all-reduce(f32[1,2,96]{2,1,0:T(2,128)S(1)} %bitcast_convert_fusion.9, f32[1,2,96]{2,1,0:T(2,128)S(1)} %bitcast_convert_fusion.8), channel_id=1, replica_groups=mesh['dp'=8,'fsdp'=4] {'dp'}, use_global_device_ids=true, to_apply=%region_49.50 | all-reduce | flops 384 | bytes 3072 | tf_op jit(solution)/shard_map/psum | solution.py:335
  600.6 65.0 %all-reduce.4.cloned.1.call-done = (f32[1,96,1152]{2,1,0:T(8,128)}, f32[1,96,1152]{2,1,0:T(8,128)}, f32[1,96,384]{2,1,0:T(8,128)}, f32[1,96,384]{2,1,0:T(8,128)}...) async-done(((f32[1,96,1152]{2,1,0:T(8,128)}, f32[1,96,1152]{2,1,0:T(8,128)}, f32[1,96,384]{2,1,0:T(8,128)}, ...) | async-done | bytes 3538960 | tf_op jit(solution)/shard_map/psum | solution.py:335
  (489 shorter events, 269.5 us)
Async XLA Ops:
  7.2 166.8 %all-gather.15.cloned.1.call-start = ((), (), s32[]{:S(2)}) async-start(), calls=%async_computation.18 | async-start | bytes 1474560 | tf_op jit(solution)/shard_map/all_gather | solution.py:190
  9.6 183.5 %all-gather.17.cloned.1.call-start = ((), (), s32[]{:S(2)}) async-start(), calls=%async_computation.19 | async-start | bytes 1474560 | tf_op jit(solution)/shard_map/all_gather | solution.py:191
  9.7 74.0 %copy-start.33 = (f32[2,96,1152]{2,1,0:T(8,128)S(1)}, f32[2,96,1152]{2,1,0:T(8,128)}, u32[]{:S(2)}) copy-start(f32[2,96,1152]{2,1,0:T(8,128)} %param.31) | copy-start | bytes 2654212
  10.6 222.1 %all-gather.19.cloned.1.call-start = ((), (), s32[]{:S(2)}) async-start(), calls=%async_computation.20 | async-start | bytes 1474560 | tf_op jit(solution)/shard_map/all_gather | solution.py:190
  11.3 240.6 %all-gather.21.cloned.1.call-start = ((), (), s32[]{:S(2)}) async-start(), calls=%async_computation.21 | async-start | bytes 1474560 | tf_op jit(solution)/shard_map/all_gather | solution.py:191
  11.9 413.2 %reduce-scatter.21.cloned.1.call-start = ((), (), s32[]{:S(2)}) async-start(), calls=%async_computation.13 | async-start | bytes 368640 | tf_op jit(solution)/shard_map/reduce_scatter | solution.py:322
  32.0 71.0 %copy-start.65 = (bf16[1024,384]{1,0:T(8,128)(2,1)S(1)}, bf16[1024,384]{1,0:T(8,128)(2,1)}, u32[]{:S(2)}) copy-start(bf16[1024,384]{1,0:T(8,128)(2,1)} %param.27) | copy-start | bytes 2359300
  49.1 86.7 %copy-start.94 = (f32[384]{0:T(512)}, f32[384]{0:T(512)S(1)}, u32[]{:S(2)}) copy-start(f32[384]{0:T(512)S(1)} %get-tuple-element.834) | copy-start | bytes 4612
  49.1 124.9 %copy-start.96 = (f32[384]{0:T(512)}, f32[384]{0:T(512)S(1)}, u32[]{:S(2)}) copy-start(f32[384]{0:T(512)S(1)} %get-tuple-element.833) | copy-start | bytes 4612
  83.7 86.6 %copy-start.44 = (bf16[1,384,384]{2,1,0:T(8,128)(2,1)}, bf16[1,384,384]{2,1,0:T(8,128)(2,1)S(1)}, u32[]{:S(2)}) copy-start(bf16[1,384,384]{2,1,0:T(8,128)(2,1)S(1)} %all-gather.2) | copy-start | bytes 884740
  103.3 67.0 %copy-start.14 = (bf16[1024,384]{0,1:T(8,128)(2,1)}, bf16[1024,384]{0,1:T(8,128)(2,1)S(1)}, u32[]{:S(2)}) copy-start(bf16[1024,384]{0,1:T(8,128)(2,1)S(1)} %copy.62) | copy-start | bytes 2359300
  267.3 159.4 %reduce-scatter.19.cloned.1.call-start = ((), (), s32[]{:S(2)}) async-start(), calls=%async_computation.12 | async-start | bytes 368640 | tf_op jit(solution)/shard_map/reduce_scatter | solution.py:322
  336.2 92.0 %reduce-scatter.17.cloned.1.call-start = ((), (), s32[]{:S(2)}) async-start(), calls=%async_computation.11 | async-start | bytes 1105920 | tf_op jit(solution)/shard_map/reduce_scatter | solution.py:319
  342.0 88.0 %reduce-scatter.15.cloned.1.call-start = ((), (), s32[]{:S(2)}) async-start(), calls=%async_computation.10 | async-start | bytes 1105920 | tf_op jit(solution)/shard_map/reduce_scatter | solution.py:319
  398.9 55.7 %reduce-scatter.29.cloned.1.call-start = ((), (), s32[]{:S(2)}) async-start(), calls=%async_computation.17 | async-start | bytes 1474560 | tf_op jit(solution)/shard_map/reduce_scatter | solution.py:328
  404.0 81.3 %reduce-scatter.25.cloned.1.call-start = ((), (), s32[]{:S(2)}) async-start(), calls=%async_computation.15 | async-start | bytes 1474560 | tf_op jit(solution)/shard_map/reduce_scatter | solution.py:325
  408.5 107.6 %reduce-scatter.23.cloned.1.call-start = ((), (), s32[]{:S(2)}) async-start(), calls=%async_computation.14 | async-start | bytes 1474560 | tf_op jit(solution)/shard_map/reduce_scatter | solution.py:325
  413.5 133.2 %reduce-scatter.27.cloned.1.call-start = ((), (), s32[]{:S(2)}) async-start(), calls=%async_computation.16 | async-start | bytes 1474560 | tf_op jit(solution)/shard_map/reduce_scatter | solution.py:328
  418.9 148.0 %reduce-scatter.33.cloned.1.call-start = ((), (), s32[]{:S(2)}) async-start(), calls=%async_computation.23 | async-start | bytes 122880
  424.1 162.8 %reduce-scatter.31.cloned.1.call-start = ((), (), s32[]{:S(2)}) async-start(), calls=%async_computation.22 | async-start | bytes 122880
  425.0 240.6 %all-reduce.4.cloned.1.call-start = ((), (), s32[]{:S(2)}) async-start(), calls=%async_computation.24 | async-start | bytes 7077888 | tf_op jit(solution)/shard_map/psum | solution.py:335
  554.0 46.0 %copy-start.104 = (f32[2,2,96]{2,1,0:T(2,128)S(1)}, f32[2,2,96]{2,1,0:T(2,128)}, u32[]{:S(2)}) copy-start(f32[2,2,96]{2,1,0:T(2,128)} %param.43) | copy-start | bytes 4612
  554.0 46.0 %copy-start.105 = (f32[2,2,96]{2,1,0:T(2,128)S(1)}, f32[2,2,96]{2,1,0:T(2,128)}, u32[]{:S(2)}) copy-start(f32[2,2,96]{2,1,0:T(2,128)} %param.45) | copy-start | bytes 4612
  554.0 46.0 %copy-start.106 = (f32[2,2,96]{2,1,0:T(2,128)S(1)}, f32[2,2,96]{2,1,0:T(2,128)}, u32[]{:S(2)}) copy-start(f32[2,2,96]{2,1,0:T(2,128)} %param.44) | copy-start | bytes 4612
  (125 other events, 662.5 us)
Sparse Core Ops, SparseCore 0:
  10.2 37.2 all-gather.14
  49.6 40.2 all-gather.16
  92.0 43.0 all-gather.18
  137.1 29.2 all-gather.20
  267.4 19.7 reduce-scatter.20
  336.3 19.7 reduce-scatter.18
  359.0 22.8 reduce-scatter.16
  399.1 24.3 reduce-scatter.14
  426.3 28.2 reduce-scatter.28
  457.4 27.8 reduce-scatter.24
  488.2 27.8 reduce-scatter.22
  518.8 27.8 reduce-scatter.26
  549.0 17.8 reduce-scatter.32
  569.6 17.2 reduce-scatter.30
  592.1 73.4 all-reduce.3
where the time goes:
time: 692 us; the launch traced here: 687 us
  waiting for transfers between devices  205 us (30%)
  matrix products  198 us (29%)
  blocking collectives  128 us (18%)
  other arithmetic  93.5 us (14%)
  local copies, waits for them, and re-layouts  42.5 us (6%)
  between operations  16.4 us (2%)
    psum x1, waiting for transfers between devices, per_device(): lax.psum((shards[0], shards[1], shards[2], shards[3], shards[4]), 'dp')  65 us
    reduce_scatter x2, waiting for transfers between devices, per_device(): lax.psum_scatter(grads[2].astype(jnp.bfloat16), 'fsdp', scatter_dimension...  57.8 us
    reduce_scatter x2, waiting for transfers between devices, per_device(): lax.psum_scatter(grads[3].astype(jnp.bfloat16), 'fsdp', scatter_dimension...  51.8 us
    all_gather x2, blocking collectives, per_device(): lax.all_gather(qkv_weight[layer_index].astype(jnp.bfloat16), 'fsdp', axis...  50.1 us
    dot_general x2, matrix products, per_device(): jnp.dot(forward_ffn_in, forward_w_up, preferred_element_type=jnp.float32)  38.2 us
    all_gather x2, blocking collectives, per_device(): lax.all_gather(proj_weight[layer_index].astype(jnp.bfloat16), 'fsdp', axi...  34.5 us
    all_gather x2, blocking collectives, per_device(): lax.all_gather(norm_gains[layer_index].astype(jnp.bfloat16), 'fsdp', axis...  31.6 us
    unnamed x17, waiting for transfers between devices  30.5 us
  transfers between devices with their start and end apart: 15, of which 7 were waited for; matrix products, arithmetic and copies ran while one was open for 42% of the time, Pallas kernels for 0%

commit v1 on v0

v1 whole, which is shorter than its diff:
```python
import functools
import math

import jax
import jax.numpy as jnp
from jax import lax
from jax.experimental import pallas as pl
from jax.experimental.pallas import tpu as pltpu
from jax.sharding import PartitionSpec as P

D = 384
HEADS = 6
HEAD_DIM = 64
FF = 1536
SEQ = 1024
STEP_COUNT = 7

NEG_FILL = -1e30
EPS_NORM = 1e-05
EPS_ADAM = 1e-08
BETA_ONE = 0.9
BETA_TWO = 0.99

LAYERS = 2
GROUPS = 4
CORES = 2
UNITS = GROUPS * CORES
BLOCK = 256
CHUNK = 512
QP, UP, DOWN = 0, 1, 2

MESH = pl.DeviceIdType.MESH
bf16 = jnp.bfloat16
f32 = jnp.float32


def dot(left, right, left_dim, right_dim):
    return lax.dot_general(
        left, right, (((left_dim,), (right_dim,)), ((), ())), preferred_element_type=f32
    )


def loop(count, body, unroll=1):
    def step(index, carry):
        body(index)
        return carry

    lax.fori_loop(0, count, step, 0, unroll=unroll)


class Remote:
    def __init__(self, src, dst, send, recv, device):
        self.made = lambda: pltpu.make_async_remote_copy(
            src_ref=src, dst_ref=dst, send_sem=send, recv_sem=recv,
            device_id=device, device_id_type=MESH,
        )

    def start(self):
        self.made().start()

    def wait_send(self):
        self.made().wait_send()

    def wait_recv(self):
        self.made().wait_recv()

    def wait(self):
        self.made().wait()


class Step:
    def __init__(self, sizes, refs):
        self.__dict__.update(sizes)
        self.__dict__.update(refs)
        self.dp = lax.axis_index("dp")
        self.z = lax.axis_index("fsdp")
        self.unit = self.dp % UNITS
        self.c = self.unit % CORES
        self.g = self.unit // CORES
        self.base = self.dp - self.unit
        self.core_peer = (self.base + self.g * CORES + (1 - self.c), self.z)
        gx, gy = self.g % 2, self.g // 2
        self.others = [gy * 2 + (1 - gx), (1 - gy) * 2 + gx, (1 - gy) * 2 + (1 - gx)]
        self.group_peers = [(self.base + g * CORES + self.c, self.z) for g in self.others]
        self.z_to = [(self.z + k) % self.Z for k in range(1, self.Z)]
        self.z_from = [(self.z + self.Z - k) % self.Z for k in range(1, self.Z)]
        self.z_peers = [(self.dp, z) for z in self.z_to]
        total = self.R * UNITS
        self.r_peers = [((self.dp + j * UNITS) % total, self.z) for j in range(1, self.R)]
        self.foreign = []
        size = 1
        while size < self.Z:
            at = self.z // size
            self.foreign.append(((at + 1 - 2 * (at % 2)) * size, size))
            size *= 2


    def remote(self, src, dst, send, recv, device):
        return Remote(src, dst, send, recv, device)

    def weight_unit(self, kind, layer, z, g, c):
        if kind == DOWN:
            return self.wdn.at[layer, z, g, c]
        whole = self.wqp if kind == QP else self.wup
        return whole.at[layer, z, c, :, pl.ds(pl.multiple_of(g * D, 128), D)]

    def weight_half(self, kind, layer, c):
        if kind == DOWN:
            return self.wdn.at[layer, :, :, c]
        return (self.wqp if kind == QP else self.wup).at[layer, :, c]

    def gather_z(self, m):
        layer, kind = divmod(m, 3)
        unit = lambda z: self.weight_unit(kind, layer, z, self.g, self.c)
        out = [
            self.remote(unit(self.z), unit(self.z), self.zs.at[m, k], self.zr.at[m, k], peer)
            for k, peer in enumerate(self.z_peers)
        ]
        into = [
            self.remote(unit(z), unit(z), self.zs.at[m, k], self.zr.at[m, k], self.z_peers[k])
            for k, z in enumerate(self.z_from)
        ]
        return out, into

    def gather_g(self, m):
        layer, kind = divmod(m, 3)
        out, into = [], []
        for k, peer in enumerate(self.group_peers):
            for b, (start, size) in enumerate(self.foreign):
                block = pl.ds(start, size)
                mine = self.weight_unit(kind, layer, block, self.g, self.c)
                theirs = self.weight_unit(kind, layer, block, self.others[k], self.c)
                i = k * len(self.foreign) + b
                out.append(self.remote(mine, mine, self.gs.at[m, i], self.gr.at[m, i], peer))
                into.append(self.remote(theirs, theirs, self.gs.at[m, i], self.gr.at[m, i], peer))
        return out, into

    def gather_c(self, m):
        layer, kind = divmod(m, 3)
        mine = self.weight_half(kind, layer, self.c)
        theirs = self.weight_half(kind, layer, 1 - self.c)
        out = self.remote(mine, mine, self.cs.at[m], self.cr.at[m], self.core_peer)
        into = self.remote(theirs, theirs, self.cs.at[m], self.cr.at[m], self.core_peer)
        return [out], [into]

    def start_z(self, m):
        for copy in self.gather_z(m)[0]:
            copy.start()

    def start_g(self, m):
        for copy in self.gather_z(m)[1]:
            copy.wait_recv()
        for copy in self.gather_g(m)[0]:
            copy.start()

    def start_c(self, m):
        for copy in self.gather_g(m)[1]:
            copy.wait_recv()
        for copy in self.gather_c(m)[0]:
            copy.start()

    def ready(self, m):
        for copy in self.gather_c(m)[1]:
            copy.wait_recv()

    def gather_sent(self):
        for m in range(3 * LAYERS):
            for copy in self.gather_z(m)[0] + self.gather_g(m)[0] + self.gather_c(m)[0]:
                copy.wait_send()


    def reduce_a(self, t):
        return self.remote(
            self.gb.at[t, :, :, 1 - self.c], self.ra.at[t],
            self.rs.at[t, 0], self.rr.at[t, 0], self.core_peer,
        )

    def reduce_b(self, t):
        return [
            self.remote(
                self.gb.at[t, self.others[k], :, self.c], self.rb.at[t, k],
                self.rs.at[t, 1 + k], self.rr.at[t, 1 + k], peer,
            )
            for k, peer in enumerate(self.group_peers)
        ]

    def reduce_c(self, m):
        layer, t = divmod(m, 3)
        return [
            self.remote(
                self.sc.at[t, self.z_to[k]], self.rc.at[layer, t, k],
                self.rs.at[t, 4 + k], self.rr.at[t, 4 + k], peer,
            )
            for k, peer in enumerate(self.z_peers)
        ]

    def reduce_r(self, m):
        layer, t = divmod(m, 3)
        return [
            self.remote(
                self.rx_out.at[layer, t], self.rx.at[layer, t, j],
                self.rxs.at[m, j], self.rxr.at[m, j], peer,
            )
            for j, peer in enumerate(self.r_peers)
        ]

    def reduce_d(self, m):
        layer, t = divmod(m, 3)
        at = 3 + self.Z
        mine = self.fin.at[layer, t, self.g, self.c]
        out, into = [], []
        for k, peer in enumerate(self.group_peers):
            theirs = self.fin.at[layer, t, self.others[k], self.c]
            sems = self.rs.at[t, at + k], self.rr.at[t, at + k]
            out.append(self.remote(mine, mine, *sems, peer))
            into.append(self.remote(theirs, theirs, *sems, peer))
        return out, into

    def reduce_e(self, m):
        layer, t = divmod(m, 3)
        sems = self.rs.at[t, 6 + self.Z], self.rr.at[t, 6 + self.Z]
        mine = self.fin.at[layer, t, :, self.c]
        theirs = self.fin.at[layer, t, :, 1 - self.c]
        return self.remote(mine, mine, *sems, self.core_peer), self.remote(
            theirs, theirs, *sems, self.core_peer
        )

    def grads_a(self, m):
        self.reduce_a(m % 3).start()

    def grads_b(self, m):
        t = m % 3
        copy = self.reduce_a(t)
        copy.wait()

        def add(g):
            both = self.gb[t, g, :, self.c].astype(f32) + self.ra[t, g].astype(f32)
            self.gb[t, g, :, self.c] = both.astype(bf16)

        loop(GROUPS, add)
        for copy in self.reduce_b(t):
            copy.start()

    def grads_c(self, m):
        t = m % 3
        for copy in self.reduce_b(t):
            copy.wait()
        total = self.gb[t, self.g, :, self.c].astype(f32)
        for k in range(GROUPS - 1):
            total = total + self.rb[t, k].astype(f32)
        self.sc[t] = total.astype(bf16)
        for copy in self.reduce_c(m):
            copy.start()

    def grads_d(self, m):
        layer, t = divmod(m, 3)
        for copy in self.reduce_c(m):
            copy.wait()
        total = self.sc[t, self.z].astype(f32)
        for k in range(self.Z - 1):
            total = total + self.rc[layer, t, k].astype(f32)
        if self.R > 1:
            self.rx_out[layer, t] = total.astype(bf16)
            for copy in self.reduce_r(m):
                copy.start()
            for copy in self.reduce_r(m):
                copy.wait()
            for j in range(self.R - 1):
                total = total + self.rx[layer, t, j].astype(f32)
        self.fin[layer, t, self.g, self.c] = total.astype(bf16)
        for copy in self.reduce_d(m)[0]:
            copy.start()

    def grads_e(self, m):
        out, into = self.reduce_d(m)
        for copy in into:
            copy.wait_recv()
        for copy in out:
            copy.wait_send()
        self.reduce_e(m)[0].start()

    def grads_f(self, m):
        layer, t = divmod(m, 3)
        out, into = self.reduce_e(m)
        into.wait_recv()
        out.wait_send()
        self.store(m).start()

    def store(self, m):
        layer, t = divmod(m, 3)
        return pltpu.make_async_copy(
            self.fin.at[layer, t], self.grads_out.at[layer, t], self.out_sem.at[2 + m]
        )


    def chunks(self, body, unroll=1):
        loop(self.T // CHUNK, lambda i: body(pl.ds(pl.multiple_of(i * CHUNK, CHUNK), CHUNK)), unroll)

    def spread(self, index):
        column = self.gcol[index]
        return jnp.concatenate([column] * (CHUNK // 128), axis=1)

    def normed(self, x, slot, at):
        mean = jnp.sum(x, axis=0, keepdims=True) * (1.0 / D)
        centered = x - mean
        inverse = lax.rsqrt(
            jnp.sum(centered * centered, axis=0, keepdims=True) * (1.0 / D) + EPS_NORM
        )
        self.stats[2 * slot : 2 * slot + 1, at] = mean
        self.stats[2 * slot + 1 : 2 * slot + 2, at] = inverse
        return centered * inverse

    def norm_back(self, grad, slot, at):
        mean = self.stats[2 * slot : 2 * slot + 1, at]
        inverse = self.stats[2 * slot + 1 : 2 * slot + 2, at]
        normed = (self.xs[slot, :, at] - mean) * inverse
        product = grad * normed
        partial = product[:, 0:128]
        for j in range(1, CHUNK // 128):
            partial = partial + product[:, j * 128 : (j + 1) * 128]
        self.gacc[slot] += partial
        gain = self.spread(slot)
        scaled = grad * gain
        average = jnp.sum(scaled, axis=0, keepdims=True) * (1.0 / D)
        along = jnp.sum(product * gain, axis=0, keepdims=True) * (1.0 / D)
        return inverse * (scaled - average - normed * along)

    def w_qkv(self, layer):
        return self.wqp[layer, :, :, :, 0 : 3 * D].reshape(D, 3 * D)

    def w_proj(self, layer):
        return self.wqp[layer, :, :, :, 3 * D : 4 * D].reshape(D, D)

    def w_up(self, layer):
        return self.wup[layer].reshape(D, FF)

    def w_down(self, layer):
        return self.wdn[layer].reshape(FF, D)

    def make_bias(self):
        prefix, valid = self.prefix[0], self.valid[0]
        key = lax.broadcasted_iota(jnp.int32, (BLOCK, BLOCK), 0)
        query = lax.broadcasted_iota(jnp.int32, (BLOCK, BLOCK), 1)
        causal = key <= query
        fill = lambda ok: jnp.where(ok, f32(0.0), f32(NEG_FILL))
        self.bias[0] = fill(causal | (key < prefix))
        self.bias[1] = fill(causal)
        self.bias[2] = fill(causal & (key + 2 * BLOCK < valid))
        self.bias[3] = fill(causal & (key + 3 * BLOCK < valid))
        self.bias[4] = fill(key + 2 * BLOCK < valid)

    def score_blocks(self, keys_t, queries, q):
        blocks = []
        for j in range(q + 1):
            s = dot(keys_t[j * BLOCK : (j + 1) * BLOCK], queries, 1, 0)
            if j == q:
                s = s + self.bias[q]
            elif j == 2:
                s = s + self.bias[4]
            blocks.append(s)
        return blocks

    def head_rows(self, h, part):
        return pl.ds(pl.multiple_of(part * D + h * HEAD_DIM, HEAD_DIM), HEAD_DIM)

    def attend(self, layer, h):
        queries = self.qkv[layer, self.head_rows(h, 0), :]
        keys_t = self.qkv[layer, self.head_rows(h, 1), :].T
        values = self.qkv[layer, self.head_rows(h, 2), :]
        values = jnp.concatenate([values, jnp.ones((16, self.T), bf16)], axis=0)
        for q in range(self.T // BLOCK):
            span = slice(q * BLOCK, (q + 1) * BLOCK)
            blocks = self.score_blocks(keys_t, queries[:, span], q)
            largest = functools.reduce(
                jnp.maximum, [jnp.max(s, axis=0, keepdims=True) for s in blocks]
            )
            probs = jnp.concatenate([jnp.exp(s - largest).astype(bf16) for s in blocks], axis=0)
            mixed = dot(values[:, : (q + 1) * BLOCK], probs, 1, 0)
            denominator = mixed[HEAD_DIM : HEAD_DIM + 1]
            mixed = mixed[:HEAD_DIM] * (1.0 / denominator)
            self.om[layer, self.head_rows(h, 0), span] = mixed.astype(bf16)
            self.lse[layer, h, :, span] = jnp.broadcast_to(
                largest + jnp.log(denominator), (8, BLOCK)
            )

    def attend_back(self, layer, h):
        queries = self.qkv[layer, self.head_rows(h, 0), :]
        keys = self.qkv[layer, self.head_rows(h, 1), :]
        keys_t = keys.T
        values_t = self.qkv[layer, self.head_rows(h, 2), :].T
        grads = self.dmix[self.head_rows(h, 0), :]
        mixed = self.om[layer, self.head_rows(h, 0), :]
        delta = jnp.sum(grads.astype(f32) * mixed.astype(f32), axis=0, keepdims=True)
        count = self.T // BLOCK
        key_grads, value_grads = [None] * count, [None] * count
        for q in range(count):
            span = slice(q * BLOCK, (q + 1) * BLOCK)
            q_rows, g_rows = queries[:, span], grads[:, span]
            blocks = self.score_blocks(keys_t, q_rows, q)
            total = self.lse[layer, h, 0:1, span]
            small = []
            for j, s in enumerate(blocks):
                probs = jnp.exp(s - total)
                slope = dot(values_t[j * BLOCK : (j + 1) * BLOCK], g_rows, 1, 0)
                low = probs.astype(bf16)
                d_scores = (probs * (slope - delta[:, span])).astype(bf16)
                small.append(d_scores)
                k_part = dot(q_rows, d_scores, 1, 1)
                v_part = dot(g_rows, low, 1, 1)
                key_grads[j] = k_part if key_grads[j] is None else key_grads[j] + k_part
                value_grads[j] = v_part if value_grads[j] is None else value_grads[j] + v_part
            d_all = jnp.concatenate(small, axis=0)
            q_part = dot(keys[:, : (q + 1) * BLOCK], d_all, 1, 0) * (HEAD_DIM**-0.5)
            self.dqkv[self.head_rows(h, 0), span] = q_part.astype(bf16)
        self.dqkv[self.head_rows(h, 1), :] = jnp.concatenate(key_grads, axis=1).astype(bf16)
        self.dqkv[self.head_rows(h, 2), :] = jnp.concatenate(value_grads, axis=1).astype(bf16)

    def first_norm(self, layer):
        slot = 2 * layer

        def body(at):
            n = self.normed(self.xs[slot, :, at], slot, at)
            self.an[layer, :, at] = (n * self.spread(slot)).astype(bf16)

        self.chunks(body)

    def project_in(self, layer):
        def body(at):
            rows = dot(self.w_qkv(layer), self.an[layer, :, at], 0, 0)
            self.qkv[layer, 0:D, at] = (rows[0:D] * (HEAD_DIM**-0.5)).astype(bf16)
            self.qkv[layer, D : 3 * D, at] = rows[D:].astype(bf16)

        self.chunks(body)

    def middle(self, layer):
        slot = 2 * layer + 1

        def body(at):
            x = self.xs[slot - 1, :, at] + dot(self.w_proj(layer), self.om[layer, :, at], 0, 0)
            self.xs[slot, :, at] = x
            n = self.normed(x, slot, at)
            self.bn[layer, :, at] = (n * self.spread(slot)).astype(bf16)

        self.chunks(body)

    def feed(self, layer):
        def body(at):
            u = dot(self.w_up(layer), self.bn[layer, :, at], 0, 0)
            area = 0.5 + 0.5 * lax.erf(u * (0.5**0.5))
            density = jnp.exp(u * u * (-0.5)) * (1.0 / math.sqrt(2.0 * math.pi))
            hidden = (u * area).astype(bf16)
            self.hid[layer, :, at] = hidden
            self.slope[layer, :, at] = (area + u * density).astype(bf16)
            x = self.xs[2 * layer + 1, :, at] + dot(self.w_down(layer), hidden, 0, 0)
            if layer + 1 < LAYERS:
                self.xs[2 * layer + 2, :, at] = x
            else:
                self.toks[at, :] = x.astype(bf16).T

        self.chunks(body)

    def feed_back(self, layer):
        slot = 2 * layer + 1

        def body(at):
            low = self.dy[:, at].astype(bf16)
            self.dm[:, at] = low
            d_hidden = dot(self.w_down(layer), low, 1, 0)
            d_pre = (d_hidden * self.slope[layer, :, at].astype(f32)).astype(bf16)
            self.slope[layer, :, at] = d_pre
            grad = dot(self.w_up(layer), d_pre, 1, 0)
            total = self.dy[:, at] + self.norm_back(grad, slot, at)
            self.dy[:, at] = total
            low = total.astype(bf16)
            self.datt[:, at] = low
            self.dmix[:, at] = dot(self.w_proj(layer), low, 1, 0).astype(bf16)

        self.chunks(body)

    def down_grad(self, layer):
        width = FF // self.Z

        def body(z):
            rows = self.hid[layer, pl.ds(pl.multiple_of(z * width, 64), width), :]
            value = dot(rows, self.dm[...], 1, 1).astype(bf16)
            self.gb[DOWN, :, z] = value.reshape(GROUPS, CORES, self.UR, D)

        loop(self.Z, body)

    def store_grad(self, t, g, value):
        self.gb[t, g] = value.astype(bf16).reshape(self.Z, CORES, self.UR, D)

    def up_grad(self, layer):
        def body(g):
            rows = self.slope[layer, pl.ds(pl.multiple_of(g * D, 64), D), :]
            self.store_grad(UP, g, dot(self.bn[layer], rows, 1, 1))

        loop(GROUPS, body)

    def proj_grad(self, layer):
        self.store_grad(QP, 3, dot(self.om[layer], self.datt[...], 1, 1))

    def qkv_grad(self, layer):
        def body(g):
            rows = self.dqkv[pl.ds(pl.multiple_of(g * D, 64), D), :]
            self.store_grad(QP, g, dot(self.an[layer], rows, 1, 1))

        loop(3, body)

    def qkv_back(self, layer):
        slot = 2 * layer

        def body(at):
            grad = dot(self.w_qkv(layer), self.dqkv[:, at], 1, 0)
            total = self.dy[:, at] + self.norm_back(grad, slot, at)
            self.dy[:, at] = total
            if layer == 0:
                self.cots[at, :] = total.astype(bf16).T

        self.chunks(body)


    def gain_slots(self):
        out, into = [], []
        for k, peer in enumerate(self.z_peers):
            mine, theirs = self.gslot.at[self.z], self.gslot.at[self.z_from[k]]
            out.append(self.remote(mine, mine, self.ns.at[k], self.nr.at[k], peer))
            into.append(self.remote(theirs, theirs, self.ns.at[k], self.nr.at[k], peer))
        return out, into

    def swap_gains(self, first, peers):
        copies = [
            self.remote(
                self.nsum.at[first], self.nin.at[first + k],
                self.ns.at[self.Z - 1 + first + k], self.nr.at[self.Z - 1 + first + k], peer,
            )
            for k, peer in enumerate(peers)
        ]
        return copies

    def fold_gains(self, first, peers, target):
        for copy in self.swap_gains(first, peers):
            copy.wait()
        total = self.nsum[first]
        for k in range(len(peers)):
            total = total + self.nin[first + k]
        self.nsum[target] = total


    def run(self):
        Z = self.Z
        loads = [
            pltpu.make_async_copy(src, dst, self.in_sem.at[i])
            for i, (src, dst) in enumerate(
                [(self.tokens, self.toks), (self.cotangent, self.cots)]
                + [
                    pair
                    for layer in range(LAYERS)
                    for pair in (
                        (self.qkv_w.at[layer, self.c], self.sq.at[layer]),
                        (self.proj_w.at[layer, self.c], self.sp.at[layer]),
                        (self.up_w.at[layer, self.c], self.su.at[layer]),
                        (self.down_w.at[layer, :, self.c], self.sd.at[layer]),
                    )
                ]
            )
        ]
        for i in (2, 3, 0, 4, 5, 6, 7, 8, 9, 1):
            loads[i].start()
        self.gslot[...] = jnp.zeros_like(self.gslot)
        for layer in range(LAYERS):
            rounded = self.gains[layer].astype(bf16).astype(f32)
            self.gslot[self.z, 2 * layer : 2 * layer + 2, 0 : D // Z] = rounded
        self.gacc[...] = jnp.zeros_like(self.gacc)

        barrier = pltpu.get_barrier_semaphore()
        peers = [self.core_peer] + self.group_peers + self.z_peers + self.r_peers
        for peer in peers:
            pl.semaphore_signal(barrier, inc=1, device_id=peer, device_id_type=MESH)
        pl.semaphore_wait(barrier, len(peers))

        for copy in self.gain_slots()[0]:
            copy.start()
        for layer in range(LAYERS):
            at = 2 + 4 * layer
            loads[at].wait()
            loads[at + 1].wait()
            self.wqp[layer, self.z, self.c, :, 0 : 3 * D] = self.sq[layer].astype(bf16)
            self.wqp[layer, self.z, self.c, :, 3 * D : 4 * D] = self.sp[layer].astype(bf16)
            self.start_z(3 * layer + QP)
            loads[at + 2].wait()
            self.wup[layer, self.z, self.c] = self.su[layer].astype(bf16)
            self.start_z(3 * layer + UP)
            loads[at + 3].wait()
            self.wdn[layer, self.z, :, self.c] = self.sd[layer].astype(bf16)
            self.start_z(3 * layer + DOWN)
        loads[0].wait()

        def take(at):
            self.xs[0, :, at] = self.toks[at, :].T.astype(f32)

        self.chunks(take)
        self.start_g(0)
        for copy in self.gain_slots()[1]:
            copy.wait_recv()
        for copy in self.gain_slots()[0]:
            copy.wait_send()
        for z in range(Z):
            tall = jnp.concatenate([self.gslot[z]] * 16, axis=0).T
            for i in range(2 * LAYERS):
                self.gcol[i, z * (D // Z) : (z + 1) * (D // Z), :] = jnp.broadcast_to(
                    tall[0 : D // Z, i : i + 1], (D // Z, 128)
                )
        self.make_bias()
        self.first_norm(0)
        self.start_g(1)
        self.start_c(0)
        self.start_g(2)
        self.ready(0)
        self.project_in(0)
        self.start_c(1)
        self.start_g(3)
        loop(HEADS, lambda h: self.attend(0, h))
        self.start_c(2)
        self.start_g(4)
        self.ready(1)
        self.middle(0)
        self.start_g(5)
        self.ready(2)
        self.feed(0)
        self.start_c(3)
        self.first_norm(1)
        self.ready(3)
        self.project_in(1)
        self.start_c(4)
        loop(HEADS, lambda h: self.attend(1, h))
        self.start_c(5)
        self.ready(4)
        self.middle(1)
        self.ready(5)
        self.feed(1)
        out_copy = pltpu.make_async_copy(self.toks, self.block_out, self.out_sem.at[0])
        out_copy.start()
        self.gather_sent()

        loads[1].wait()
        valid = self.valid[0]

        def start_back(at):
            where = at.start + lax.broadcasted_iota(jnp.int32, (D, CHUNK), 1)
            grad = self.cots[at, :].T.astype(f32)
            self.dy[:, at] = jnp.where(where < valid, grad, f32(0.0))

        self.chunks(start_back)

        self.feed_back(1)
        self.down_grad(1)
        self.grads_a(5)
        self.up_grad(1)
        self.grads_a(4)
        self.proj_grad(1)
        self.grads_b(5)

        def heads_one(h):
            self.attend_back(1, h)
            pl.when(h == 0)(lambda: self.grads_b(4))
            pl.when(h == 1)(lambda: self.grads_c(5))
            pl.when(h == 2)(lambda: self.grads_c(4))
            pl.when(h == 3)(lambda: self.grads_d(5))
            pl.when(h == 4)(lambda: self.grads_d(4))

        loop(HEADS, heads_one)
        self.grads_e(5)
        self.grads_e(4)
        self.qkv_grad(1)
        self.grads_a(3)
        self.qkv_back(1)

        self.feed_back(0)
        self.grads_b(3)
        self.down_grad(0)
        self.grads_f(5)
        self.grads_a(2)
        self.up_grad(0)
        self.grads_f(4)
        self.grads_a(1)
        self.grads_c(3)
        self.proj_grad(0)
        self.grads_b(2)

        def heads_zero(h):
            self.attend_back(0, h)
            pl.when(h == 0)(lambda: self.grads_d(3))
            pl.when(h == 1)(lambda: self.grads_b(1))
            pl.when(h == 2)(lambda: self.grads_c(2))
            pl.when(h == 2)(lambda: self.grads_e(3))
            pl.when(h == 3)(lambda: self.grads_c(1))
            pl.when(h == 4)(lambda: self.grads_d(2))

        loop(HEADS, heads_zero)
        self.grads_d(1)
        self.grads_f(3)
        self.qkv_grad(0)
        self.grads_a(0)
        self.grads_e(2)
        self.grads_e(1)
        self.qkv_back(0)
        grad_copy = pltpu.make_async_copy(self.cots, self.tokens_grad, self.out_sem.at[1])
        grad_copy.start()
        self.grads_b(0)

        lane = lax.broadcasted_iota(jnp.int32, (D, 128), 1)
        tall = jnp.zeros((D, 128), f32)
        for i in range(2 * LAYERS):
            column = jnp.sum(self.gacc[i], axis=1, keepdims=True)
            tall = tall + jnp.where(lane == i, column, f32(0.0))
        self.nsum[0] = tall.T[0:8]
        stages = [[self.core_peer], self.group_peers, self.z_peers]
        if self.R > 1:
            stages.append(self.r_peers)
        firsts = [0, 1, 1 + len(self.group_peers), 1 + len(self.group_peers) + Z - 1]
        last = firsts[len(stages) - 1] + len(stages[-1])
        ends = firsts[1 : len(stages)] + [last]
        for copy in self.swap_gains(0, stages[0]):
            copy.start()
        self.fold_gains(0, stages[0], ends[0])
        for copy in self.swap_gains(firsts[1], stages[1]):
            copy.start()
        self.grads_f(2)
        self.grads_f(1)
        self.grads_c(0)
        for i in range(1, len(stages)):
            self.fold_gains(firsts[i], stages[i], ends[i])
            if i + 1 < len(stages):
                for copy in self.swap_gains(firsts[i + 1], stages[i + 1]):
                    copy.start()
        self.grads_d(0)
        tall = jnp.concatenate([self.nsum[last]] * 16, axis=0).T
        self.gcol[0] = tall
        width = D // Z
        mine = self.gcol[0, pl.ds(pl.multiple_of(self.z * width, 8), width), :]
        mine = jnp.concatenate([mine, jnp.zeros((128 - width, 128), f32)], axis=0).T
        self.gains_grad[...] = mine[0:8]
        self.grads_e(0)
        self.grads_f(0)
        out_copy.wait()
        grad_copy.wait()
        for m in range(3 * LAYERS):
            self.store(m).wait()


def adam(weight, first, second, grad, rate, decay):
    first_new = BETA_ONE * first + (1.0 - BETA_ONE) * grad
    second_new = BETA_TWO * second + (1.0 - BETA_TWO) * grad * grad
    first_fix = 1.0 - BETA_ONE**STEP_COUNT
    second_fix = 1.0 - BETA_TWO**STEP_COUNT
    update = first_new / first_fix / (jnp.sqrt(second_new / second_fix) + EPS_ADAM)
    return first_new, second_new, weight - rate * (update + decay * weight)


def adam_kernel(*refs):
    (block_in, tgrad_in, grads, gains_grad) = refs[:4]
    masters = refs[4:19]
    block_out, tgrad_out = refs[19:21]
    outs = refs[21:]
    rates = (
        2.5 / math.sqrt(D),
        2.5 / math.sqrt(max(4 * D // SEQ, 1)),
        2.5 / math.sqrt(D),
        2.5 / math.sqrt(FF),
        0.5,
    )
    block_out[...] = block_in[...]
    tgrad_out[...] = tgrad_in[...]

    def update(kind, index, grad):
        weight, first, second = (masters[3 * kind + j] for j in range(3))
        new = adam(
            weight[index], first[index], second[index], grad, rates[kind],
            0.1 if kind < 4 else 0.0,
        )
        for j in range(3):
            outs[3 * kind + j][index] = new[j]

    for g in range(GROUPS):
        grad = grads[0, QP, g, 0].astype(f32)
        if g < 3:
            update(0, (0, 0, slice(None), slice(g * D, (g + 1) * D)), grad)
        else:
            update(1, (0, 0), grad)
        update(2, (0, 0, slice(None), slice(g * D, (g + 1) * D)), grads[0, UP, g, 0].astype(f32))
        update(3, (0, g, 0), grads[0, DOWN, g, 0].astype(f32))
    width = masters[12].shape[-1]
    for layer in range(LAYERS):
        update(4, (layer,), gains_grad[2 * layer : 2 * layer + 2, 0:width])


def make_per_device(n_dp, n_fsdp):
    Z, R = n_fsdp, n_dp // UNITS
    UR = D // Z // CORES

    def per_device(
        tokens, cotangent, prefix_len, valid_len,
        qkv_weight, qkv_first, qkv_second,
        proj_weight, proj_first, proj_second,
        up_weight, up_first, up_second,
        down_weight, down_first, down_second,
        norm_gains, gains_first, gains_second,
    ):
        T = tokens.shape[0]
        assert prefix_len.shape == (1,) and T == 4 * BLOCK
        assert FF // Z // UNITS == UR
        rows4 = lambda w: w.reshape(LAYERS, CORES, UR, w.shape[-1])
        rows5 = lambda w: w.reshape(LAYERS, GROUPS, CORES, UR, D)
        vmem = pltpu.VMEM
        scratch = dict(
            wqp=vmem((LAYERS, Z, CORES, UR, 4 * D), bf16),
            wup=vmem((LAYERS, Z, CORES, UR, FF), bf16),
            wdn=vmem((LAYERS, Z, GROUPS, CORES, UR, D), bf16),
            sq=vmem((LAYERS, UR, 3 * D), f32),
            sp=vmem((LAYERS, UR, D), f32),
            su=vmem((LAYERS, UR, FF), f32),
            sd=vmem((LAYERS, GROUPS, UR, D), f32),
            gslot=vmem((Z, 8, 128), f32),
            gcol=vmem((2 * LAYERS, D, 128), f32),
            gacc=vmem((2 * LAYERS, D, 128), f32),
            xs=vmem((2 * LAYERS, D, T), f32),
            dy=vmem((D, T), f32),
            an=vmem((LAYERS, D, T), bf16),
            bn=vmem((LAYERS, D, T), bf16),
            qkv=vmem((LAYERS, 3 * D, T), bf16),
            om=vmem((LAYERS, D, T), bf16),
            hid=vmem((LAYERS, FF, T), bf16),
            slope=vmem((LAYERS, FF, T), bf16),
            dqkv=vmem((3 * D, T), bf16),
            dmix=vmem((D, T), bf16),
            dm=vmem((D, T), bf16),
            datt=vmem((D, T), bf16),
            lse=vmem((LAYERS, HEADS, 8, T), f32),
            stats=vmem((4 * LAYERS, T), f32),
            bias=vmem((5, BLOCK, BLOCK), f32),
            toks=vmem((T, D), bf16),
            cots=vmem((T, D), bf16),
            gb=vmem((3, GROUPS, Z, CORES, UR, D), bf16),
            ra=vmem((3, GROUPS, Z, UR, D), bf16),
            rb=vmem((3, GROUPS - 1, Z, UR, D), bf16),
            sc=vmem((3, Z, UR, D), bf16),
            rc=vmem((LAYERS, 3, Z - 1, UR, D), bf16),
            fin=vmem((LAYERS, 3, GROUPS, CORES, UR, D), bf16),
            nsum=vmem((8 + Z + R, 8, D), f32),
            nin=vmem((8 + Z + R, 8, D), f32),
        )
        sem = pltpu.SemaphoreType.DMA
        levels = Z.bit_length() - 1
        scratch.update(
            zs=sem((3 * LAYERS, Z - 1)),
            zr=sem((3 * LAYERS, Z - 1)),
            gs=sem((3 * LAYERS, 3 * levels)),
            gr=sem((3 * LAYERS, 3 * levels)),
            cs=sem((3 * LAYERS,)),
            cr=sem((3 * LAYERS,)),
            rs=sem((3, 7 + Z)),
            rr=sem((3, 7 + Z)),
            ns=sem((2 * Z + R + 4,)),
            nr=sem((2 * Z + R + 4,)),
            in_sem=sem((2 + 4 * LAYERS,)),
            out_sem=sem((2 + 3 * LAYERS,)),
        )
        if R > 1:
            scratch.update(
                rx=vmem((LAYERS, 3, R - 1, UR, D), bf16),
                rx_out=vmem((LAYERS, 3, UR, D), bf16),
                rxs=sem((3 * LAYERS, R - 1)),
                rxr=sem((3 * LAYERS, R - 1)),
            )
        ins = dict(
            tokens=tokens, cotangent=cotangent, prefix=prefix_len, valid=valid_len,
            qkv_w=rows4(qkv_weight), proj_w=rows4(proj_weight), up_w=rows4(up_weight),
            down_w=rows5(down_weight), gains=norm_gains,
        )
        outs = dict(
            block_out=jax.ShapeDtypeStruct((T, D), bf16),
            tokens_grad=jax.ShapeDtypeStruct((T, D), bf16),
            grads_out=jax.ShapeDtypeStruct((LAYERS, 3, GROUPS, CORES, UR, D), bf16),
            gains_grad=jax.ShapeDtypeStruct((8, 128), f32),
        )
        names = list(ins) + list(outs) + list(scratch)
        hbm = pl.BlockSpec(memory_space=pl.ANY)
        smem = pl.BlockSpec(memory_space=pltpu.SMEM)
        local = pl.BlockSpec(memory_space=pltpu.VMEM)

        def kernel(*refs):
            Step(dict(T=T, Z=Z, R=R, UR=UR), dict(zip(names, refs))).run()

        block_mid, tgrad_mid, grads, gains_grad = pl.pallas_call(
            kernel,
            out_shape=list(outs.values()),
            in_specs=[hbm, hbm, smem, smem, hbm, hbm, hbm, hbm, local],
            out_specs=[hbm, hbm, hbm, local],
            scratch_shapes=list(scratch.values()),
            compiler_params=pltpu.CompilerParams(
                collective_id=0, has_side_effects=True, vmem_limit_bytes=62 * 1024 * 1024
            ),
            name="train_step",
        )(*ins.values())

        masters = [
            f(w)
            for f, group in (
                (rows4, (qkv_weight, qkv_first, qkv_second)),
                (rows4, (proj_weight, proj_first, proj_second)),
                (rows4, (up_weight, up_first, up_second)),
                (rows5, (down_weight, down_first, down_second)),
                (lambda w: w, (norm_gains, gains_first, gains_second)),
            )
            for w in group
        ]
        tok_block = pl.BlockSpec((T // 4, D), lambda l, c: (2 * l + c, 0))

        def spec(w):
            if w.ndim == 4:
                return pl.BlockSpec((1, 1, *w.shape[2:]), lambda l, c: (l, c, 0, 0))
            if w.ndim == 5:
                return pl.BlockSpec((1, GROUPS, 1, UR, D), lambda l, c: (l, 0, c, 0, 0))
            return pl.BlockSpec(w.shape, lambda l, c: (0, 0, 0))

        specs = [spec(w) for w in masters]
        done = pl.pallas_call(
            adam_kernel,
            grid=(LAYERS, CORES),
            out_shape=[jax.ShapeDtypeStruct((T, D), bf16)] * 2
            + [jax.ShapeDtypeStruct(w.shape, f32) for w in masters],
            in_specs=[
                tok_block,
                tok_block,
                pl.BlockSpec((1, 3, GROUPS, 1, UR, D), lambda l, c: (l, 0, 0, c, 0, 0)),
                pl.BlockSpec((8, 128), lambda l, c: (0, 0)),
                *specs,
            ],
            out_specs=[tok_block, tok_block, *specs],
            compiler_params=pltpu.CompilerParams(vmem_limit_bytes=48 * 1024 * 1024),
            name="adam",
        )(block_mid, tgrad_mid, grads, gains_grad, *masters)
        shapes = [
            w.shape
            for w in (
                qkv_weight, qkv_first, qkv_second, proj_weight, proj_first, proj_second,
                up_weight, up_first, up_second, down_weight, down_first, down_second,
                norm_gains, gains_first, gains_second,
            )
        ]
        news = [x.reshape(s) for x, s in zip(done[2:], shapes)]
        results = []
        for kind in range(5):
            weight_new, second_new, first_new = news[3 * kind + 2], news[3 * kind + 1], news[3 * kind]
            results += [first_new, second_new, weight_new]
        return (done[0], done[1], *results)

    return per_device


def solution(mesh):
    rows = P(("dp", "fsdp"), None)
    lens = P(("dp", "fsdp"))
    weight = P(None, "fsdp", None)
    gain = P(None, None, "fsdp")
    return jax.shard_map(
        make_per_device(mesh.shape["dp"], mesh.shape["fsdp"]),
        mesh=mesh,
        in_specs=(rows, rows, lens, lens, *([weight] * 12), *([gain] * 3)),
        out_specs=(rows, rows, *([weight] * 12), *([gain] * 3)),
        check_vma=False,
    )
```

time: 692 us -> 180 us (0.26)
  waiting for transfers between devices: 205 us -> 0 us
  matrix products: 198 us -> 0 us
  Pallas kernels: 0 us -> 172 us
  blocking collectives: 128 us -> 0 us
  other arithmetic: 93.5 us -> 0 us
  local copies, waits for them, and re-layouts: 42.5 us -> 5.29 us
  between operations: 16.4 us -> 2.26 us
    dot_general x52 -> x0, matrix products: 198 us -> none  [the longest x2 38.2 us: per_device(): jnp.dot(forward_ffn_in, forward_w_up, preferred_element_type=jnp.float32)]
    pallas_call x0 -> x2, Pallas kernels: none -> 172 us  [the longest x1 163 us: per_device(): pl.pallas_call(kernel, out_shape=list(outs.values()), in_specs=[hbm, hbm,...]
    all_gather x6 -> x0, blocking collectives: 116 us -> none  [the longest x2 50.1 us: per_device(): lax.all_gather(qkv_weight[layer_index].astype(jnp.bfloat16), 'fsdp', axis...]
    reduce_scatter x8 -> x0, waiting for transfers between devices: 110 us -> none  [the longest x2 57.8 us: per_device(): lax.psum_scatter(grads[2].astype(jnp.bfloat16), 'fsdp', scatter_dimension...]
    psum x1 -> x0, waiting for transfers between devices: 65 us -> none  [per_device(): lax.psum((shards[0], shards[1], shards[2], shards[3], shards[4]), 'dp')]
    unnamed x17 -> x0, waiting for transfers between devices: 30.5 us -> none
    convert_element_type x5 -> x0, other arithmetic: 29.7 us -> none  [the longest x4 27.8 us: per_sequence(): grad_scores = (soft_probs * (grad_probs - jnp.sum(grad_probs * soft_probs...]
    unnamed x226 -> x24, local copies, waits for them, and re-layouts: 26.7 us -> 5.29 us
  transfers between devices with their start and end apart: 15 -> 0, of which waited for: 7 -> 0; matrix products, arithmetic and copies ran while one was open for 42% -> 0% of each run, Pallas kernels for 0% -> 0%
where the time goes in v1:
time: 180 us
  Pallas kernels  172 us (96%)
  local copies, waits for them, and re-layouts  5.29 us (3%)
  between operations  2.26 us (1%)
    pallas_call x1, Pallas kernels, per_device(): pl.pallas_call(kernel, out_shape=list(outs.values()), in_specs=[hbm, hbm,...  163 us
    pallas_call x1, Pallas kernels, per_device(): pl.pallas_call(adam_kernel, grid=(LAYERS, CORES), out_shape=[jax.ShapeDty...  8.94 us
    unnamed x24, local copies, waits for them, and re-layouts  5.29 us

profile of v1, /device:TPU:0, one launch (start us, length us, event | category | flops | bytes accessed | tf_op | source)
XLA Modules:
  0.0 179.6 jit_solution(11292585130460070853)
XLA Ops:
  1.9 0.0 copy-start
  2.0 0.0 copy-start.1
  2.0 0.0 copy-start.6
  2.0 0.0 copy-start.7
  2.0 0.0 copy-start.8
  2.0 0.0 copy-start.10
  2.0 0.0 copy-start.11
  2.0 163.1 %train_step.1 = (bf16[1024,384]{1,0:T(8,128)(2,1)}, bf16[1024,384]{1,0:T(8,128)(2,1)}, bf16[2,3,4,2,48,384]{5,4,3,2,1,0:T(8,128)(2,1)}, f32[8,128]{1,0:T(8,128)}) custom-call(bf16[1024,384]{1,0:T(8,128)(2,1)} %refs_0_.1, bf16[1024,384]{1,0:T(8,128)(2,1)} %refs_1_.1, s32[1]{0:T(128)S(6)} %copy.36.refs_2_, s32[1]{0:T(128)S(6)} %copy.37.refs_3_, ...), custom_call_target="tpu_custom_call" | custom-call | tf_op jit(solution)/shard_map/train_step/pallas_call | solution.py:895
  165.1 0.0 copy-done
  165.1 0.0 copy-done.1
  165.1 0.0 copy-done.6
  165.1 0.0 copy-done.7
  165.1 0.0 copy-done.8
  165.2 0.0 copy-done.10
  165.2 0.0 copy-done.11
  165.2 0.0 copy-start.2
  165.2 1.2 copy-done.2
  166.3 0.0 copy-start.3
  166.4 1.2 copy-done.3
  167.5 0.0 copy-start.4
  167.5 1.1 copy-done.4
  168.7 1.1 copy-done.5
  169.8 0.7 copy-done.9
  170.5 8.9 %adam.1 = (bf16[1024,384]{1,0:T(8,128)(2,1)}, bf16[1024,384]{1,0:T(8,128)(2,1)}, f32[2,2,48,1152]{3,2,1,0:T(8,128)}, f32[2,2,48,1152]{3,2,1,0:T(8,128)}, f32[2,2...) custom-call(bf16[1024,384]{1,0:T(8,128)(2,1)S(1)} %copy-done.4, ...), custom_call_target="tpu_custom_call" | custom-call | tf_op jit(solution)/shard_map/adam/pallas_call | solution.py:928
  (2 shorter events, 0.0 us)
Async XLA Ops:
  1.9 163.2 %copy-start = (f32[2,96,1152]{2,1,0:T(8,128)S(1)}, f32[2,96,1152]{2,1,0:T(8,128)}, u32[]{:S(2)}) copy-start(f32[2,96,1152]{2,1,0:T(8,128)} %param.23) | copy-start | bytes 2654212
  2.0 163.2 %copy-start.1 = (f32[2,96,384]{2,1,0:T(8,128)S(1)}, f32[2,96,384]{2,1,0:T(8,128)}, u32[]{:S(2)}) copy-start(f32[2,96,384]{2,1,0:T(8,128)} %param.26) | copy-start | bytes 884740
  2.0 163.2 %copy-start.6 = (f32[2,96,384]{2,1,0:T(8,128)S(1)}, f32[2,96,384]{2,1,0:T(8,128)}, u32[]{:S(2)}) copy-start(f32[2,96,384]{2,1,0:T(8,128)} %param.27) | copy-start | bytes 884740
  2.0 163.2 %copy-start.7 = (f32[2,96,384]{2,1,0:T(8,128)S(1)}, f32[2,96,384]{2,1,0:T(8,128)}, u32[]{:S(2)}) copy-start(f32[2,96,384]{2,1,0:T(8,128)} %param.28) | copy-start | bytes 884740
  2.0 163.2 %copy-start.8 = (f32[2,2,96]{2,1,0:T(2,128)S(1)}, f32[2,2,96]{2,1,0:T(2,128)}, u32[]{:S(2)}) copy-start(f32[2,2,96]{2,1,0:T(2,128)} %refs_16_.1) | copy-start | bytes 4612
  2.0 163.2 %copy-start.10 = (f32[2,2,96]{2,1,0:T(2,128)S(1)}, f32[2,2,96]{2,1,0:T(2,128)}, u32[]{:S(2)}) copy-start(f32[2,2,96]{2,1,0:T(2,128)} %refs_17_.1) | copy-start | bytes 4612
  2.0 163.2 %copy-start.11 = (f32[2,2,96]{2,1,0:T(2,128)S(1)}, f32[2,2,96]{2,1,0:T(2,128)}, u32[]{:S(2)}) copy-start(f32[2,2,96]{2,1,0:T(2,128)} %refs_18_.1) | copy-start | bytes 4612
  165.2 1.2 copy-start.2
  166.3 1.2 copy-start.3
  167.5 1.1 copy-start.4
  168.7 1.1 copy-start.5
  169.8 0.7 copy-start.9

commit v2 on v1

v2 whole, which is shorter than its diff:
```python
import functools
import math

import jax
import jax.numpy as jnp
from jax import lax
from jax.experimental import pallas as pl
from jax.experimental.pallas import tpu as pltpu
from jax.sharding import PartitionSpec as P

D = 384
HEADS = 6
HEAD_DIM = 64
FF = 1536
SEQ = 1024
STEP_COUNT = 7

NEG_FILL = -1e30
EPS_NORM = 1e-05
EPS_ADAM = 1e-08
BETA_ONE = 0.9
BETA_TWO = 0.99

LAYERS = 2
GROUPS = 4
CORES = 2
UNITS = GROUPS * CORES
BLOCK = 256
CHUNK = 512
QP, UP, DOWN = 0, 1, 2
PAIR = 2 * HEAD_DIM
ITEMS = [(layer, kind, kind, pl.ds(0, D)) for layer, kind in ((1, DOWN), (1, UP), (1, QP), (0, DOWN), (0, UP))]
ITEMS += [(0, QP, 3, pl.ds(p * PAIR, PAIR)) for p in range(3)]
D1, U1, Q1, D0, U0, P0, P1, P2 = range(8)
LAST = P2

MESH = pl.DeviceIdType.MESH
bf16 = jnp.bfloat16
f32 = jnp.float32


def dot(left, right, left_dim, right_dim):
    return lax.dot_general(
        left, right, (((left_dim,), (right_dim,)), ((), ())), preferred_element_type=f32
    )


def loop(count, body, unroll=1):
    def step(index, carry):
        body(index)
        return carry

    lax.fori_loop(0, count, step, 0, unroll=unroll)


class Remote:
    def __init__(self, src, dst, send, recv, device):
        self.made = lambda: pltpu.make_async_remote_copy(
            src_ref=src, dst_ref=dst, send_sem=send, recv_sem=recv,
            device_id=device, device_id_type=MESH,
        )

    def start(self):
        self.made().start()

    def wait_send(self):
        self.made().wait_send()

    def wait_recv(self):
        self.made().wait_recv()

    def wait(self):
        self.made().wait()


class Step:
    def __init__(self, sizes, refs):
        self.__dict__.update(sizes)
        self.__dict__.update(refs)
        self.dp = lax.axis_index("dp")
        self.z = lax.axis_index("fsdp")
        self.unit = self.dp % UNITS
        self.c = self.unit % CORES
        self.g = self.unit // CORES
        self.base = self.dp - self.unit
        self.core_peer = (self.base + self.g * CORES + (1 - self.c), self.z)
        gx, gy = self.g % 2, self.g // 2
        self.gx, self.gy = gx, gy
        self.others = [gy * 2 + (1 - gx), (1 - gy) * 2 + gx, (1 - gy) * 2 + (1 - gx)]
        self.group_peers = [(self.base + g * CORES + self.c, self.z) for g in self.others]
        self.z_others = []
        for k in range(1, self.Z):
            other, bit = 0, 1
            while bit < self.Z:
                own = (self.z // bit) % 2
                other = other + bit * (1 - own if k & bit else own)
                bit *= 2
            self.z_others.append(other)
        self.z_peers = [(self.dp, z) for z in self.z_others]
        total = self.R * UNITS
        self.r_peers = [((self.dp + j * UNITS) % total, self.z) for j in range(1, self.R)]


    def remote(self, src, dst, send, recv, device):
        return Remote(src, dst, send, recv, device)

    def weight_unit(self, kind, layer, z, g, c):
        if kind == DOWN:
            return self.wdn.at[layer, z, g, c]
        whole = self.wqp if kind == QP else self.wup
        return whole.at[layer, z, c, :, pl.ds(pl.multiple_of(g * D, 128), D)]

    def weight_half(self, kind, layer, z, c):
        if kind == DOWN:
            return self.wdn.at[layer, z, :, c]
        return (self.wqp if kind == QP else self.wup).at[layer, z, c]

    def gather_z(self, m):
        layer, kind = divmod(m, 3)
        unit = lambda z: self.weight_unit(kind, layer, z, self.g, self.c)
        out, into = [], []
        for k, peer in enumerate(self.z_peers):
            sems = self.zs.at[m, k], self.zr.at[m, k]
            out.append(self.remote(unit(self.z), unit(self.z), *sems, peer))
            into.append(self.remote(unit(self.z_others[k]), unit(self.z_others[k]), *sems, peer))
        return out, into

    def gather_g(self, m, k):
        layer, kind = divmod(m, 3)
        unit = lambda g: self.weight_unit(kind, layer, self.z_others[k], g, self.c)
        out, into = [], []
        for j, peer in enumerate(self.group_peers):
            sems = self.gs.at[m, 3 * k + j], self.gr.at[m, 3 * k + j]
            out.append(self.remote(unit(self.g), unit(self.g), *sems, peer))
            into.append(self.remote(unit(self.others[j]), unit(self.others[j]), *sems, peer))
        return out, into

    def gather_c(self, m, k):
        layer, kind = divmod(m, 3)
        z = self.z if k == self.Z - 1 else self.z_others[k]
        half = lambda c: self.weight_half(kind, layer, z, c)
        sems = self.cs.at[m, k], self.cr.at[m, k]
        out = self.remote(half(self.c), half(self.c), *sems, self.core_peer)
        into = self.remote(half(1 - self.c), half(1 - self.c), *sems, self.core_peer)
        return out, into

    def start_z(self, m):
        for copy in self.gather_z(m)[0]:
            copy.start()
        self.gather_c(m, self.Z - 1)[0].start()

    def start_g(self, m):
        into = self.gather_z(m)[1]
        for k in range(self.Z - 1):
            into[k].wait_recv()
            for copy in self.gather_g(m, k)[0]:
                copy.start()

    def start_c(self, m):
        for k in range(self.Z - 1):
            for copy in self.gather_g(m, k)[1]:
                copy.wait_recv()
            self.gather_c(m, k)[0].start()

    def ready(self, m):
        for k in range(self.Z):
            self.gather_c(m, k)[1].wait_recv()

    def gather_sent(self):
        for m in range(3 * LAYERS):
            copies = self.gather_z(m)[0] + [self.gather_c(m, k)[0] for k in range(self.Z)]
            for k in range(self.Z - 1):
                copies += self.gather_g(m, k)[0]
            for copy in copies:
                copy.wait_send()


    def reduce_a(self, i):
        layer, t, buf, cols = ITEMS[i]
        return [
            self.remote(
                self.gb.at[t, :, :, :, 1 - self.c, :, cols], self.ra.at[buf, :, :, :, :, cols],
                self.rs.at[i, 0], self.rr.at[i, 0], self.core_peer,
            )
        ]

    def reduce_b1(self, i):
        layer, t, buf, cols = ITEMS[i]
        half = self.Z // 2
        return [
            self.remote(
                self.gb.at[t, :, 1 - self.gx, 0:half, self.c, :, cols],
                self.rb1.at[buf, 0, :, :, :, cols],
                self.rs.at[i, 1], self.rr.at[i, 1], self.group_peers[0],
            ),
            self.remote(
                self.gb.at[t, 1 - self.gy, :, half:, self.c, :, cols],
                self.rb1.at[buf, 1, :, :, :, cols],
                self.rs.at[i, 2], self.rr.at[i, 2], self.group_peers[1],
            ),
        ]

    def reduce_b2(self, i):
        layer, t, buf, cols = ITEMS[i]
        half = self.Z // 2
        return [
            self.remote(
                self.gb.at[t, 1 - self.gy, self.gx, 0:half, self.c, :, cols],
                self.rb2.at[buf, 0, :, :, cols],
                self.rs.at[i, 3], self.rr.at[i, 3], self.group_peers[1],
            ),
            self.remote(
                self.gb.at[t, self.gy, 1 - self.gx, half:, self.c, :, cols],
                self.rb2.at[buf, 1, :, :, cols],
                self.rs.at[i, 4], self.rr.at[i, 4], self.group_peers[0],
            ),
        ]

    def reduce_b(self, i):
        layer, t, buf, cols = ITEMS[i]
        return [
            self.remote(
                self.gb.at[t, self.others[k] // 2, self.others[k] % 2, :, self.c, :, cols],
                self.rb.at[k],
                self.rs.at[i, 1 + k], self.rr.at[i, 1 + k], peer,
            )
            for k, peer in enumerate(self.group_peers)
        ]

    def reduce_c(self, i):
        layer, t, buf, cols = ITEMS[i]
        return [
            self.remote(
                self.sc.at[buf, self.z_others[k], :, cols], self.rc.at[layer, t, k, :, cols],
                self.rs.at[i, 5 + k], self.rr.at[i, 5 + k], peer,
            )
            for k, peer in enumerate(self.z_peers)
        ]

    def reduce_r(self, i):
        layer, t, buf, cols = ITEMS[i]
        return [
            self.remote(
                self.rx_out.at[layer, t, :, cols], self.rx.at[layer, t, j, :, cols],
                self.rxs.at[i, j], self.rxr.at[i, j], peer,
            )
            for j, peer in enumerate(self.r_peers)
        ]

    def reduce_d(self, i):
        layer, t, buf, cols = ITEMS[i]
        at = 4 + self.Z
        mine = self.fin.at[layer, t, self.g, self.c, :, cols]
        out, into = [], []
        for k, peer in enumerate(self.group_peers):
            theirs = self.fin.at[layer, t, self.others[k], self.c, :, cols]
            sems = self.rs.at[i, at + k], self.rr.at[i, at + k]
            out.append(self.remote(mine, mine, *sems, peer))
            into.append(self.remote(theirs, theirs, *sems, peer))
        return out, into

    def reduce_e(self, i):
        layer, t, buf, cols = ITEMS[i]
        sems = self.rs.at[i, 7 + self.Z], self.rr.at[i, 7 + self.Z]
        mine = self.fin.at[layer, t, :, self.c, :, cols]
        theirs = self.fin.at[layer, t, :, 1 - self.c, :, cols]
        return [self.remote(mine, mine, *sems, self.core_peer)], [
            self.remote(theirs, theirs, *sems, self.core_peer)
        ]

    def each(self, copies, action):
        for copy in copies:
            getattr(copy, action)()

    def grads_a(self, i):
        self.each(self.reduce_a(i), "start")

    def add_cores(self, i):
        layer, t, buf, cols = ITEMS[i]
        self.each(self.reduce_a(i), "wait")

        def add(g):
            at = (t, g // 2, g % 2, slice(None), self.c, slice(None), cols)
            both = self.gb[at].astype(f32) + self.ra[buf, g // 2, g % 2, :, :, cols].astype(f32)
            self.gb[at] = both.astype(bf16)

        loop(GROUPS, add)

    def grads_b1(self, i):
        self.add_cores(i)
        self.each(self.reduce_b1(i), "start")

    def grads_b2(self, i):
        layer, t, buf, cols = ITEMS[i]
        half = self.Z // 2
        self.each(self.reduce_b1(i), "wait")
        at = (t, slice(None), self.gx, slice(0, half), self.c, slice(None), cols)
        both = self.gb[at].astype(f32) + self.rb1[buf, 0, :, :, :, cols].astype(f32)
        self.gb[at] = both.astype(bf16)
        at = (t, self.gy, slice(None), slice(half, self.Z), self.c, slice(None), cols)
        both = self.gb[at].astype(f32) + self.rb1[buf, 1, :, :, :, cols].astype(f32)
        self.gb[at] = both.astype(bf16)
        self.each(self.reduce_b2(i), "start")

    def grads_b(self, i):
        self.add_cores(i)
        self.each(self.reduce_b(i), "start")

    def grads_c(self, i):
        layer, t, buf, cols = ITEMS[i]
        half = self.Z // 2
        if i == LAST:
            self.each(self.reduce_b(i), "wait")
            total = self.gb[t, self.gy, self.gx, :, self.c, :, cols].astype(f32)
            for k in range(GROUPS - 1):
                total = total + self.rb[k].astype(f32)
            self.sc[buf, :, :, cols] = total.astype(bf16)
        else:
            self.each(self.reduce_b2(i), "wait")
            for j in range(2):
                span = slice(j * half, (j + 1) * half)
                total = self.gb[t, self.gy, self.gx, span, self.c, :, cols].astype(f32)
                total = total + self.rb2[buf, j, :, :, cols].astype(f32)
                self.sc[buf, span, :, cols] = total.astype(bf16)
        self.each(self.reduce_c(i), "start")

    def grads_d(self, i):
        layer, t, buf, cols = ITEMS[i]
        self.each(self.reduce_c(i), "wait")
        total = self.sc[buf, self.z, :, cols].astype(f32)
        for k in range(self.Z - 1):
            total = total + self.rc[layer, t, k, :, cols].astype(f32)
        if self.R > 1:
            self.rx_out[layer, t, :, cols] = total.astype(bf16)
            self.each(self.reduce_r(i), "start")
            self.each(self.reduce_r(i), "wait")
            for j in range(self.R - 1):
                total = total + self.rx[layer, t, j, :, cols].astype(f32)
        self.fin[layer, t, self.g, self.c, :, cols] = total.astype(bf16)
        self.each(self.reduce_d(i)[0], "start")

    def grads_e(self, i):
        out, into = self.reduce_d(i)
        self.each(into, "wait_recv")
        self.each(out, "wait_send")
        self.each(self.reduce_e(i)[0], "start")

    def grads_f(self, i):
        out, into = self.reduce_e(i)
        self.each(into, "wait_recv")
        self.each(out, "wait_send")
        if ITEMS[i][2] < 3:
            self.store(*ITEMS[i][:2]).start()

    def store(self, layer, t):
        return pltpu.make_async_copy(
            self.fin.at[layer, t], self.grads_out.at[layer, t], self.out_sem.at[2 + 3 * layer + t]
        )


    def chunks(self, body, unroll=1):
        loop(self.T // CHUNK, lambda i: body(pl.ds(pl.multiple_of(i * CHUNK, CHUNK), CHUNK)), unroll)

    def spread(self, index):
        column = self.gcol[index].astype(f32)
        return jnp.concatenate([column] * (CHUNK // 128), axis=1)

    def normed(self, x, slot, at):
        mean = jnp.sum(x, axis=0, keepdims=True) * (1.0 / D)
        centered = x - mean
        inverse = lax.rsqrt(
            jnp.sum(centered * centered, axis=0, keepdims=True) * (1.0 / D) + EPS_NORM
        )
        self.stats[2 * slot : 2 * slot + 1, at] = mean
        self.stats[2 * slot + 1 : 2 * slot + 2, at] = inverse
        return centered * inverse

    def norm_back(self, grad, slot, at):
        mean = self.stats[2 * slot : 2 * slot + 1, at]
        inverse = self.stats[2 * slot + 1 : 2 * slot + 2, at]
        normed = (self.xs[slot, :, at] - mean) * inverse
        product = grad * normed
        partial = product[:, 0:128]
        for j in range(1, CHUNK // 128):
            partial = partial + product[:, j * 128 : (j + 1) * 128]
        self.gacc[slot] += partial
        gain = self.spread(slot)
        scaled = grad * gain
        average = jnp.sum(scaled, axis=0, keepdims=True) * (1.0 / D)
        along = jnp.sum(product * gain, axis=0, keepdims=True) * (1.0 / D)
        return inverse * (scaled - average - normed * along)

    def w_qkv(self, layer):
        return self.wqp[layer, :, :, :, 0 : 3 * D].reshape(D, 3 * D)

    def w_proj(self, layer):
        return self.wqp[layer, :, :, :, 3 * D : 4 * D].reshape(D, D)

    def w_up(self, layer):
        return self.wup[layer].reshape(D, FF)

    def w_down(self, layer):
        return self.wdn[layer].reshape(FF, D)

    def make_bias(self):
        prefix, valid = self.prefix[0], self.valid[0]
        key = lax.broadcasted_iota(jnp.int32, (BLOCK, BLOCK), 0)
        query = lax.broadcasted_iota(jnp.int32, (BLOCK, BLOCK), 1)
        causal = key <= query
        fill = lambda ok: jnp.where(ok, f32(0.0), f32(NEG_FILL))
        self.bias[0] = fill(causal | (key < prefix))
        self.bias[1] = fill(causal)
        self.bias[2] = fill(causal & (key + 2 * BLOCK < valid))
        self.bias[3] = fill(causal & (key + 3 * BLOCK < valid))
        self.bias[4] = fill(key + 2 * BLOCK < valid)

    def score_blocks(self, keys_t, queries, q):
        blocks = []
        for j in range(q + 1):
            s = dot(keys_t[j * BLOCK : (j + 1) * BLOCK], queries, 1, 0)
            if j == q:
                s = s + self.bias[q]
            elif j == 2:
                s = s + self.bias[4]
            blocks.append(s)
        return blocks

    def head_rows(self, h, part):
        return pl.ds(pl.multiple_of(part * D + h * HEAD_DIM, HEAD_DIM), HEAD_DIM)

    def attend(self, layer, heads):
        count = self.T // BLOCK
        span = lambda q: slice(q * BLOCK, (q + 1) * BLOCK)
        queries = [self.qkv[layer, self.head_rows(h, 0), :] for h in heads]
        keys_t = [self.qkv[layer, self.head_rows(h, 1), :].T for h in heads]
        ones = jnp.ones((16, self.T), bf16)
        values = [
            jnp.concatenate([self.qkv[layer, self.head_rows(h, 2), :], ones], axis=0) for h in heads
        ]

        def scores(a, q):
            return self.score_blocks(keys_t[a], queries[a][:, span(q)], q)

        def soften(blocks):
            largest = functools.reduce(
                jnp.maximum, [jnp.max(s, axis=0, keepdims=True) for s in blocks]
            )
            probs = jnp.concatenate([jnp.exp(s - largest).astype(bf16) for s in blocks], axis=0)
            return largest, probs

        def mix(a, q, largest, probs):
            mixed = dot(values[a][:, : (q + 1) * BLOCK], probs, 1, 0)
            denominator = mixed[HEAD_DIM : HEAD_DIM + 1]
            mixed = mixed[:HEAD_DIM] * (1.0 / denominator)
            self.om[layer, self.head_rows(heads[a], 0), span(q)] = mixed.astype(bf16)
            self.lse[layer, pl.ds(heads[a], 1), span(q)] = largest + jnp.log(denominator)

        self.pipeline(len(heads), range(count), scores, lambda a, q, s: soften(s), mix)

    def pipeline(self, n, order, first, second, third):
        work = [(a, q) for q in order for a in range(n)]
        now = first(*work[0])
        last = None
        for i, place in enumerate(work):
            ahead = first(*work[i + 1]) if i + 1 < len(work) else None
            made = second(*place, now)
            if last is not None:
                third(*last[0], *last[1])
            last, now = (place, made), ahead
        third(*last[0], *last[1])

    def attend_back(self, layer, heads):
        count = self.T // BLOCK
        span = lambda q: slice(q * BLOCK, (q + 1) * BLOCK)
        part = lambda i: [self.qkv[layer, self.head_rows(h, i), :] for h in heads]
        queries, keys, values = part(0), part(1), part(2)
        keys_t, values_t = [k.T for k in keys], [v.T for v in values]
        grads = [self.dmix[self.head_rows(h, 0), :] for h in heads]
        delta = [
            jnp.sum(
                g.astype(f32) * self.om[layer, self.head_rows(h, 0), :].astype(f32),
                axis=0, keepdims=True,
            )
            for g, h in zip(grads, heads)
        ]
        key_grads = [[None] * count for h in heads]
        value_grads = [[None] * count for h in heads]

        def first(a, q):
            scores = self.score_blocks(keys_t[a], queries[a][:, span(q)], q)
            slopes = [dot(values_t[a][span(j)], grads[a][:, span(q)], 1, 0) for j in range(q + 1)]
            return scores, slopes

        def second(a, q, made):
            total = self.lse[layer, pl.ds(heads[a], 1), span(q)]
            low, small = [], []
            for s, slope in zip(*made):
                probs = jnp.exp(s - total)
                low.append(probs.astype(bf16))
                small.append((probs * (slope - delta[a][:, span(q)])).astype(bf16))
            return jnp.concatenate(low, axis=0), jnp.concatenate(small, axis=0)

        def third(a, q, probs, d_scores):
            k_part = dot(queries[a][:, span(q)], d_scores, 1, 1)
            v_part = dot(grads[a][:, span(q)], probs, 1, 1)
            for j in range(q + 1):
                for grad, more in ((key_grads[a], k_part), (value_grads[a], v_part)):
                    grad[j] = more[:, span(j)] if grad[j] is None else grad[j] + more[:, span(j)]
            q_part = dot(keys[a][:, : (q + 1) * BLOCK], d_scores, 1, 0) * (HEAD_DIM**-0.5)
            self.dqkv[self.head_rows(heads[a], 0), span(q)] = q_part.astype(bf16)

        self.pipeline(len(heads), reversed(range(count)), first, second, third)
        for a, h in enumerate(heads):
            self.dqkv[self.head_rows(h, 1), :] = jnp.concatenate(key_grads[a], axis=1).astype(bf16)
            self.dqkv[self.head_rows(h, 2), :] = jnp.concatenate(value_grads[a], axis=1).astype(bf16)

    def first_norm(self, layer):
        slot = 2 * layer

        def body(at):
            n = self.normed(self.xs[slot, :, at], slot, at)
            self.an[layer, :, at] = (n * self.spread(slot)).astype(bf16)

        self.chunks(body)

    def project_in(self, layer):
        def body(at):
            rows = dot(self.w_qkv(layer), self.an[layer, :, at], 0, 0)
            self.qkv[layer, 0:D, at] = (rows[0:D] * (HEAD_DIM**-0.5)).astype(bf16)
            self.qkv[layer, D : 3 * D, at] = rows[D:].astype(bf16)

        self.chunks(body)

    def middle(self, layer):
        slot = 2 * layer + 1

        def body(at):
            x = self.xs[slot - 1, :, at] + dot(self.w_proj(layer), self.om[layer, :, at], 0, 0)
            self.xs[slot, :, at] = x
            n = self.normed(x, slot, at)
            self.bn[layer, :, at] = (n * self.spread(slot)).astype(bf16)

        self.chunks(body)

    def feed(self, layer):
        def body(at):
            u = dot(self.w_up(layer), self.bn[layer, :, at], 0, 0)
            area = 0.5 + 0.5 * lax.erf(u * (0.5**0.5))
            density = jnp.exp(u * u * (-0.5)) * (1.0 / math.sqrt(2.0 * math.pi))
            hidden = (u * area).astype(bf16)
            self.hid[layer, :, at] = hidden
            self.slope[layer, :, at] = (area + u * density).astype(bf16)
            x = self.xs[2 * layer + 1, :, at] + dot(self.w_down(layer), hidden, 0, 0)
            if layer + 1 < LAYERS:
                self.xs[2 * layer + 2, :, at] = x
            else:
                self.toks[at, :] = x.astype(bf16).T

        self.chunks(body)

    def feed_back(self, layer):
        slot = 2 * layer + 1

        def body(at):
            low = self.dy[:, at].astype(bf16)
            self.dm[:, at] = low
            d_hidden = dot(self.w_down(layer), low, 1, 0)
            d_pre = (d_hidden * self.slope[layer, :, at].astype(f32)).astype(bf16)
            self.slope[layer, :, at] = d_pre
            grad = dot(self.w_up(layer), d_pre, 1, 0)
            total = self.dy[:, at] + self.norm_back(grad, slot, at)
            self.dy[:, at] = total
            low = total.astype(bf16)
            self.datt[:, at] = low
            self.dmix[:, at] = dot(self.w_proj(layer), low, 1, 0).astype(bf16)

        self.chunks(body)

    def down_grad(self, layer):
        width = FF // self.Z

        def body(z):
            rows = self.hid[layer, pl.ds(pl.multiple_of(z * width, 64), width), :]
            value = dot(rows, self.dm[...], 1, 1).astype(bf16)
            self.gb[DOWN, :, :, z] = value.reshape(2, 2, CORES, self.UR, D)

        loop(self.Z, body)

    def store_grad(self, t, g, value):
        self.gb[t, g // 2, g % 2] = value.astype(bf16).reshape(self.Z, CORES, self.UR, D)

    def up_grad(self, layer):
        def body(g):
            rows = self.slope[layer, pl.ds(pl.multiple_of(g * D, 64), D), :]
            self.store_grad(UP, g, dot(self.bn[layer], rows, 1, 1))

        loop(GROUPS, body)

    def proj_grad(self, layer):
        self.store_grad(QP, 3, dot(self.om[layer], self.datt[...], 1, 1))

    def qkv_grad(self, layer):
        def body(g):
            rows = self.dqkv[pl.ds(pl.multiple_of(g * D, 64), D), :]
            self.store_grad(QP, g, dot(self.an[layer], rows, 1, 1))

        loop(3, body)

    def pair_grad(self, p):
        rows = [self.dqkv[g * D + p * PAIR : g * D + (p + 1) * PAIR, :] for g in range(3)]
        value = dot(self.an[0], jnp.concatenate(rows, axis=0), 1, 1).astype(bf16)
        value = value.reshape(self.Z, CORES, self.UR, 3 * PAIR)
        for g in range(3):
            part = value[:, :, :, g * PAIR : (g + 1) * PAIR]
            self.gb[QP, g // 2, g % 2, :, :, :, p * PAIR : (p + 1) * PAIR] = part

    def qkv_back(self, layer):
        slot = 2 * layer

        def body(at):
            grad = dot(self.w_qkv(layer), self.dqkv[:, at], 1, 0)
            total = self.dy[:, at] + self.norm_back(grad, slot, at)
            self.dy[:, at] = total
            if layer == 0:
                self.cots[at, :] = total.astype(bf16).T

        self.chunks(body)


    def gain_slots(self):
        out, into = [], []
        for k, peer in enumerate(self.z_peers):
            mine, theirs = self.gslot.at[self.z], self.gslot.at[self.z_others[k]]
            out.append(self.remote(mine, mine, self.ns.at[k], self.nr.at[k], peer))
            into.append(self.remote(theirs, theirs, self.ns.at[k], self.nr.at[k], peer))
        return out, into

    def gain_stages(self):
        stages = [[self.core_peer], self.group_peers, self.z_peers]
        return stages + [self.r_peers] if self.R > 1 else stages

    def swap_gains(self, stage):
        stages = self.gain_stages()
        at = sum(len(peers) for peers in stages[:stage])
        return [
            self.remote(
                self.nsum.at[stage], self.nin.at[at + k],
                self.ns.at[self.Z - 1 + at + k], self.nr.at[self.Z - 1 + at + k], peer,
            )
            for k, peer in enumerate(stages[stage])
        ]

    def fold_gains(self, stage):
        stages = self.gain_stages()
        at = sum(len(peers) for peers in stages[:stage])
        self.each(self.swap_gains(stage), "wait")
        total = self.nsum[stage]
        for k in range(len(stages[stage])):
            total = total + self.nin[at + k]
        self.nsum[stage + 1] = total
        if stage + 1 < len(stages):
            self.each(self.swap_gains(stage + 1), "start")


    def run(self):
        Z = self.Z
        loads = [
            pltpu.make_async_copy(src, dst, self.in_sem.at[i])
            for i, (src, dst) in enumerate(
                [(self.tokens, self.toks), (self.cotangent, self.cots)]
                + [
                    pair
                    for layer in range(LAYERS)
                    for pair in (
                        (self.qkv_w.at[layer, self.c], self.sq),
                        (self.proj_w.at[layer, self.c], self.sp),
                        (self.up_w.at[layer, self.c], self.su),
                        (self.down_w.at[layer, :, self.c], self.sd),
                    )
                ]
            )
        ]
        for i in (2, 3, 0, 4, 5, 1):
            loads[i].start()
        self.gslot[...] = jnp.zeros_like(self.gslot)
        for layer in range(LAYERS):
            rounded = self.gains[layer].astype(bf16).astype(f32)
            self.gslot[self.z, 2 * layer : 2 * layer + 2, 0 : D // Z] = rounded
        self.gacc[...] = jnp.zeros_like(self.gacc)

        def take_weights(m):
            layer, kind = divmod(m, 3)
            at = 2 + 4 * layer
            parts = [at, at + 1] if kind == QP else [at + 1 + kind]
            for i in parts:
                loads[i].wait()
            if kind == QP:
                self.wqp[layer, self.z, self.c, :, 0 : 3 * D] = self.sq[...].astype(bf16)
                self.wqp[layer, self.z, self.c, :, 3 * D : 4 * D] = self.sp[...].astype(bf16)
            elif kind == UP:
                self.wup[layer, self.z, self.c] = self.su[...].astype(bf16)
            else:
                self.wdn[layer, self.z, :, self.c] = self.sd[...].astype(bf16)
            if layer + 1 < LAYERS:
                for i in parts:
                    loads[i + 4].start()

        take_weights(0)
        barrier = pltpu.get_barrier_semaphore()
        peers = [self.core_peer] + self.group_peers + self.z_peers + self.r_peers
        for peer in peers:
            pl.semaphore_signal(barrier, inc=1, device_id=peer, device_id_type=MESH)
        pl.semaphore_wait(barrier, len(peers))

        self.start_z(0)
        for copy in self.gain_slots()[0]:
            copy.start()
        loads[0].wait()

        def take(at):
            self.xs[0, :, at] = self.toks[at, :].T.astype(f32)

        self.chunks(take)
        self.start_g(0)
        take_weights(1)
        self.start_z(1)
        take_weights(2)
        self.start_z(2)
        for copy in self.gain_slots()[1]:
            copy.wait_recv()
        for copy in self.gain_slots()[0]:
            copy.wait_send()
        for z in range(Z):
            tall = jnp.concatenate([self.gslot[z]] * 16, axis=0).T
            for i in range(2 * LAYERS):
                self.gcol[i, z * (D // Z) : (z + 1) * (D // Z), :] = jnp.broadcast_to(
                    tall[0 : D // Z, i : i + 1], (D // Z, 128)
                ).astype(bf16)
        self.first_norm(0)
        self.start_c(0)
        self.make_bias()
        for m in range(3, 3 * LAYERS):
            take_weights(m)
        self.start_g(1)
        self.start_z(3)
        self.ready(0)
        self.project_in(0)
        self.start_g(2)
        self.start_z(4)
        self.start_z(5)

        def heads(body, layer, n, hooks):
            def step(i):
                body(layer, [n * i + a for a in range(n)])
                for at, hook in hooks:
                    pl.when(i == at)(hook)

            loop(HEADS // n, step)

        def do(f, *args):
            return lambda: f(*args)

        heads(self.attend, 0, 3, [(0, do(self.start_g, 3)), (1, do(self.start_c, 1))])
        self.start_g(4)
        self.ready(1)
        self.middle(0)
        self.start_c(2)
        self.start_g(5)
        self.ready(2)
        self.feed(0)
        self.start_c(3)
        self.first_norm(1)
        self.ready(3)
        self.project_in(1)
        heads(self.attend, 1, 3, [(0, do(self.start_c, 4)), (1, do(self.start_c, 5))])
        self.ready(4)
        self.middle(1)
        self.ready(5)
        self.feed(1)
        out_copy = pltpu.make_async_copy(self.toks, self.block_out, self.out_sem.at[0])
        out_copy.start()
        self.gather_sent()

        loads[1].wait()
        valid = self.valid[0]

        def start_back(at):
            where = at.start + lax.broadcasted_iota(jnp.int32, (D, CHUNK), 1)
            grad = self.cots[at, :].T.astype(f32)
            self.dy[:, at] = jnp.where(where < valid, grad, f32(0.0))

        self.chunks(start_back)

        self.feed_back(1)
        self.down_grad(1)
        self.grads_a(D1)
        self.up_grad(1)
        self.grads_a(U1)
        self.grads_b1(D1)
        self.proj_grad(1)
        heads(
            self.attend_back, 1, 2,
            [
                (0, do(self.grads_b1, U1)),
                (1, do(self.grads_b2, D1)),
                (2, do(self.grads_b2, U1)),
                (2, do(self.grads_c, D1)),
            ],
        )
        self.grads_c(U1)
        self.qkv_grad(1)
        self.grads_a(Q1)
        self.grads_d(D1)
        self.qkv_back(1)
        self.grads_b1(Q1)

        self.feed_back(0)
        self.grads_d(U1)
        self.grads_e(D1)
        self.grads_b2(Q1)
        self.down_grad(0)
        self.grads_f(D1)
        self.grads_a(D0)
        self.up_grad(0)
        self.grads_e(U1)
        self.grads_c(Q1)
        self.grads_b1(D0)
        self.proj_grad(0)
        heads(
            self.attend_back, 0, 2,
            [
                (0, do(self.pair_grad, 0)),
                (0, do(self.grads_a, P0)),
                (0, do(self.grads_f, U1)),
                (0, do(self.grads_a, U0)),
                (0, do(self.grads_d, Q1)),
                (1, do(self.pair_grad, 1)),
                (1, do(self.grads_a, P1)),
                (1, do(self.grads_b2, D0)),
                (1, do(self.grads_b1, U0)),
                (1, do(self.grads_b1, P0)),
                (2, do(self.pair_grad, 2)),
                (2, do(self.grads_a, P2)),
                (2, do(self.grads_e, Q1)),
                (2, do(self.grads_b2, U0)),
                (2, do(self.grads_c, D0)),
                (2, do(self.grads_b1, P1)),
                (2, do(self.grads_b2, P0)),
                (2, do(self.grads_b, P2)),
            ],
        )
        self.qkv_back(0)
        grad_copy = pltpu.make_async_copy(self.cots, self.tokens_grad, self.out_sem.at[1])
        grad_copy.start()

        lane = lax.broadcasted_iota(jnp.int32, (D, 128), 1)
        tall = jnp.zeros((D, 128), f32)
        for i in range(2 * LAYERS):
            column = jnp.sum(self.gacc[i], axis=1, keepdims=True)
            tall = tall + jnp.where(lane == i, column, f32(0.0))
        self.nsum[0] = tall.T[0:8]
        self.each(self.swap_gains(0), "start")
        self.grads_b2(P1)
        self.grads_c(U0)
        self.grads_c(P0)
        self.fold_gains(0)
        self.grads_f(Q1)
        self.grads_c(P2)
        self.grads_d(D0)
        self.grads_c(P1)
        self.grads_d(U0)
        self.fold_gains(1)
        self.grads_e(D0)
        self.grads_d(P0)
        self.grads_d(P2)
        self.grads_d(P1)
        self.grads_e(U0)
        self.fold_gains(2)
        if self.R > 1:
            self.fold_gains(3)
        tall = jnp.concatenate([self.nsum[len(self.gain_stages())]] * 16, axis=0).T
        self.gacc[0] = tall
        width = D // Z
        mine = self.gacc[0, pl.ds(pl.multiple_of(self.z * width, 8), width), :]
        mine = jnp.concatenate([mine, jnp.zeros((128 - width, 128), f32)], axis=0).T
        self.gains_grad[...] = mine[0:8]
        self.grads_f(D0)
        self.grads_f(U0)
        for i in (P0, P2, P1):
            self.grads_e(i)
        for i in (P0, P2, P1):
            self.grads_f(i)
        self.store(0, QP).start()
        out_copy.wait()
        grad_copy.wait()
        for layer in range(LAYERS):
            for t in range(3):
                self.store(layer, t).wait()


def adam(weight, first, second, grad, rate, decay):
    first_new = BETA_ONE * first + (1.0 - BETA_ONE) * grad
    second_new = BETA_TWO * second + (1.0 - BETA_TWO) * grad * grad
    first_fix = 1.0 - BETA_ONE**STEP_COUNT
    second_fix = 1.0 - BETA_TWO**STEP_COUNT
    update = first_new / first_fix / (jnp.sqrt(second_new / second_fix) + EPS_ADAM)
    return first_new, second_new, weight - rate * (update + decay * weight)


def adam_kernel(*refs):
    (block_in, tgrad_in, grads, gains_grad) = refs[:4]
    masters = refs[4:19]
    block_out, tgrad_out = refs[19:21]
    outs = refs[21:]
    rates = (
        2.5 / math.sqrt(D),
        2.5 / math.sqrt(max(4 * D // SEQ, 1)),
        2.5 / math.sqrt(D),
        2.5 / math.sqrt(FF),
        0.5,
    )
    block_out[...] = block_in[...]
    tgrad_out[...] = tgrad_in[...]

    def update(kind, index, grad):
        weight, first, second = (masters[3 * kind + j] for j in range(3))
        new = adam(
            weight[index], first[index], second[index], grad, rates[kind],
            0.1 if kind < 4 else 0.0,
        )
        for j in range(3):
            outs[3 * kind + j][index] = new[j]

    for g in range(GROUPS):
        grad = grads[0, QP, g, 0].astype(f32)
        if g < 3:
            update(0, (0, 0, slice(None), slice(g * D, (g + 1) * D)), grad)
        else:
            update(1, (0, 0), grad)
        update(2, (0, 0, slice(None), slice(g * D, (g + 1) * D)), grads[0, UP, g, 0].astype(f32))
        update(3, (0, g, 0), grads[0, DOWN, g, 0].astype(f32))
    width = masters[12].shape[-1]
    for layer in range(LAYERS):
        update(4, (layer,), gains_grad[2 * layer : 2 * layer + 2, 0:width])


def make_per_device(n_dp, n_fsdp):
    Z, R = n_fsdp, n_dp // UNITS
    UR = D // Z // CORES

    def per_device(
        tokens, cotangent, prefix_len, valid_len,
        qkv_weight, qkv_first, qkv_second,
        proj_weight, proj_first, proj_second,
        up_weight, up_first, up_second,
        down_weight, down_first, down_second,
        norm_gains, gains_first, gains_second,
    ):
        T = tokens.shape[0]
        assert prefix_len.shape == (1,) and T == 4 * BLOCK
        assert FF // Z // UNITS == UR
        rows4 = lambda w: w.reshape(LAYERS, CORES, UR, w.shape[-1])
        rows5 = lambda w: w.reshape(LAYERS, GROUPS, CORES, UR, D)
        vmem = pltpu.VMEM
        scratch = dict(
            wqp=vmem((LAYERS, Z, CORES, UR, 4 * D), bf16),
            wup=vmem((LAYERS, Z, CORES, UR, FF), bf16),
            wdn=vmem((LAYERS, Z, GROUPS, CORES, UR, D), bf16),
            sq=vmem((UR, 3 * D), f32),
            sp=vmem((UR, D), f32),
            su=vmem((UR, FF), f32),
            sd=vmem((GROUPS, UR, D), f32),
            gslot=vmem((Z, 8, 128), f32),
            gcol=vmem((2 * LAYERS, D, 128), bf16),
            gacc=vmem((2 * LAYERS, D, 128), f32),
            xs=vmem((2 * LAYERS, D, T), f32),
            dy=vmem((D, T), f32),
            an=vmem((LAYERS, D, T), bf16),
            bn=vmem((LAYERS, D, T), bf16),
            qkv=vmem((LAYERS, 3 * D, T), bf16),
            om=vmem((LAYERS, D, T), bf16),
            hid=vmem((LAYERS, FF, T), bf16),
            slope=vmem((LAYERS, FF, T), bf16),
            dqkv=vmem((3 * D, T), bf16),
            dmix=vmem((D, T), bf16),
            dm=vmem((D, T), bf16),
            datt=vmem((D, T), bf16),
            lse=vmem((LAYERS, 8, T), f32),
            stats=vmem((4 * LAYERS, T), f32),
            bias=vmem((5, BLOCK, BLOCK), f32),
            toks=vmem((T, D), bf16),
            cots=vmem((T, D), bf16),
            gb=vmem((3, 2, 2, Z, CORES, UR, D), bf16),
            ra=vmem((4, 2, 2, Z, UR, D), bf16),
            rb1=vmem((4, 2, 2, Z // 2, UR, D), bf16),
            rb2=vmem((4, 2, Z // 2, UR, D), bf16),
            rb=vmem((GROUPS - 1, Z, UR, PAIR), bf16),
            sc=vmem((4, Z, UR, D), bf16),
            rc=vmem((LAYERS, 3, Z - 1, UR, D), bf16),
            fin=vmem((LAYERS, 3, GROUPS, CORES, UR, D), bf16),
            nsum=vmem((5, 8, D), f32),
            nin=vmem((GROUPS + Z + R - 2, 8, D), f32),
        )
        sem = pltpu.SemaphoreType.DMA
        scratch.update(
            zs=sem((3 * LAYERS, Z - 1)),
            zr=sem((3 * LAYERS, Z - 1)),
            gs=sem((3 * LAYERS, 3 * (Z - 1))),
            gr=sem((3 * LAYERS, 3 * (Z - 1))),
            cs=sem((3 * LAYERS, Z)),
            cr=sem((3 * LAYERS, Z)),
            rs=sem((len(ITEMS), 8 + Z)),
            rr=sem((len(ITEMS), 8 + Z)),
            ns=sem((2 * Z + R + 4,)),
            nr=sem((2 * Z + R + 4,)),
            in_sem=sem((2 + 4 * LAYERS,)),
            out_sem=sem((2 + 3 * LAYERS,)),
        )
        if R > 1:
            scratch.update(
                rx=vmem((LAYERS, 3, R - 1, UR, D), bf16),
                rx_out=vmem((LAYERS, 3, UR, D), bf16),
                rxs=sem((len(ITEMS), R - 1)),
                rxr=sem((len(ITEMS), R - 1)),
            )
        ins = dict(
            tokens=tokens, cotangent=cotangent, prefix=prefix_len, valid=valid_len,
            qkv_w=rows4(qkv_weight), proj_w=rows4(proj_weight), up_w=rows4(up_weight),
            down_w=rows5(down_weight), gains=norm_gains,
        )
        outs = dict(
            block_out=jax.ShapeDtypeStruct((T, D), bf16),
            tokens_grad=jax.ShapeDtypeStruct((T, D), bf16),
            grads_out=jax.ShapeDtypeStruct((LAYERS, 3, GROUPS, CORES, UR, D), bf16),
            gains_grad=jax.ShapeDtypeStruct((8, 128), f32),
        )
        names = list(ins) + list(outs) + list(scratch)
        hbm = pl.BlockSpec(memory_space=pl.ANY)
        smem = pl.BlockSpec(memory_space=pltpu.SMEM)
        local = pl.BlockSpec(memory_space=pltpu.VMEM)

        def kernel(*refs):
            Step(dict(T=T, Z=Z, R=R, UR=UR), dict(zip(names, refs))).run()

        block_mid, tgrad_mid, grads, gains_grad = pl.pallas_call(
            kernel,
            out_shape=list(outs.values()),
            in_specs=[hbm, hbm, smem, smem, hbm, hbm, hbm, hbm, local],
            out_specs=[hbm, hbm, hbm, local],
            scratch_shapes=list(scratch.values()),
            compiler_params=pltpu.CompilerParams(
                collective_id=0, has_side_effects=True, vmem_limit_bytes=63 * 1024 * 1024
            ),
            name="train_step",
        )(*ins.values())

        masters = [
            f(w)
            for f, group in (
                (rows4, (qkv_weight, qkv_first, qkv_second)),
                (rows4, (proj_weight, proj_first, proj_second)),
                (rows4, (up_weight, up_first, up_second)),
                (rows5, (down_weight, down_first, down_second)),
                (lambda w: w, (norm_gains, gains_first, gains_second)),
            )
            for w in group
        ]
        tok_block = pl.BlockSpec((T // 4, D), lambda l, c: (2 * l + c, 0))

        def spec(w):
            if w.ndim == 4:
                return pl.BlockSpec((1, 1, *w.shape[2:]), lambda l, c: (l, c, 0, 0))
            if w.ndim == 5:
                return pl.BlockSpec((1, GROUPS, 1, UR, D), lambda l, c: (l, 0, c, 0, 0))
            return pl.BlockSpec(w.shape, lambda l, c: (0, 0, 0))

        specs = [spec(w) for w in masters]
        done = pl.pallas_call(
            adam_kernel,
            grid=(LAYERS, CORES),
            out_shape=[jax.ShapeDtypeStruct((T, D), bf16)] * 2
            + [jax.ShapeDtypeStruct(w.shape, f32) for w in masters],
            in_specs=[
                tok_block,
                tok_block,
                pl.BlockSpec((1, 3, GROUPS, 1, UR, D), lambda l, c: (l, 0, 0, c, 0, 0)),
                pl.BlockSpec((8, 128), lambda l, c: (0, 0)),
                *specs,
            ],
            out_specs=[tok_block, tok_block, *specs],
            compiler_params=pltpu.CompilerParams(vmem_limit_bytes=62 * 1024 * 1024),
            name="adam",
        )(block_mid, tgrad_mid, grads, gains_grad, *masters)
        shapes = [
            w.shape
            for w in (
                qkv_weight, qkv_first, qkv_second, proj_weight, proj_first, proj_second,
                up_weight, up_first, up_second, down_weight, down_first, down_second,
                norm_gains, gains_first, gains_second,
            )
        ]
        news = [x.reshape(s) for x, s in zip(done[2:], shapes)]
        results = []
        for kind in range(5):
            weight_new, second_new, first_new = news[3 * kind + 2], news[3 * kind + 1], news[3 * kind]
            results += [first_new, second_new, weight_new]
        return (done[0], done[1], *results)

    return per_device


def solution(mesh):
    rows = P(("dp", "fsdp"), None)
    lens = P(("dp", "fsdp"))
    weight = P(None, "fsdp", None)
    gain = P(None, None, "fsdp")
    return jax.shard_map(
        make_per_device(mesh.shape["dp"], mesh.shape["fsdp"]),
        mesh=mesh,
        in_specs=(rows, rows, lens, lens, *([weight] * 12), *([gain] * 3)),
        out_specs=(rows, rows, *([weight] * 12), *([gain] * 3)),
        check_vma=False,
    )
```

time: 180 us -> 143 us (0.79)
  Pallas kernels: 172 us -> 141 us
  local copies, waits for them, and re-layouts: 5.29 us -> 0 us
    pallas_call x1, Pallas kernels: 163 us -> 131 us  [per_device(): pl.pallas_call(kernel, out_shape=list(outs.values()), in_specs=[hbm, hbm,...]
    unnamed x24 -> x0, local copies, waits for them, and re-layouts: 5.29 us -> none
where the time goes in v2:
time: 143 us
  Pallas kernels  141 us (99%)
  between operations  2.14 us (1%)
    pallas_call x1, Pallas kernels, per_device(): pl.pallas_call(kernel, out_shape=list(outs.values()), in_specs=[hbm, hbm,...  131 us
    pallas_call x1, Pallas kernels, per_device(): pl.pallas_call(adam_kernel, grid=(LAYERS, CORES), out_shape=[jax.ShapeDty...  10.1 us

profile of v2, /device:TPU:0, one launch (start us, length us, event | category | flops | bytes accessed | tf_op | source)
XLA Modules:
  0.0 142.8 jit_solution(7058320991085094656)
XLA Ops:
  1.9 130.6 %train_step.1 = (bf16[1024,384]{1,0:T(8,128)(2,1)}, bf16[1024,384]{1,0:T(8,128)(2,1)}, bf16[2,3,4,2,48,384]{5,4,3,2,1,0:T(8,128)(2,1)}, f32[8,128]{1,0:T(8,128)}) custom-call(bf16[1024,384]{1,0:T(8,128)(2,1)} %refs_0_.1, bf16[1024,384]{1,0:T(8,128)(2,1)} %refs_1_.1, s32[1]{0:T(128)S(6)} %copy.36.refs_2_, s32[1]{0:T(128)S(6)} %copy.37.refs_3_, ...), custom_call_target="tpu_custom_call" | custom-call | tf_op jit(solution)/shard_map/train_step/pallas_call | solution.py:1045
  132.5 10.1 %adam.1 = (bf16[1024,384]{1,0:T(8,128)(2,1)}, bf16[1024,384]{1,0:T(8,128)(2,1)}, f32[2,2,48,1152]{3,2,1,0:T(8,128)}, f32[2,2,48,1152]{3,2,1,0:T(8,128)}, f32[2,2...) custom-call(bf16[1024,384]{1,0:T(8,128)(2,1)} %get-tuple-element.38., ...), custom_call_target="tpu_custom_call" | custom-call | tf_op jit(solution)/shard_map/adam/pallas_call | solution.py:1078
